TPU v7x, 32 devices: a whole 2x2x4 slice. The times are simulated.
32 devices in a mesh: expert: 16 (over z, y, x), half: 1, dp: 2 (over core).
Axes of the slice: x: 2, y: 2, z: 4, core: 2. Of those that a mesh axis runs over, the one named last changes fastest.
Arguments:
- tokens: bfloat16 [4096, 4096], P(('expert', 'dp'), 'half'), may hold values from -6 to 6
- cotangent: bfloat16 [4096, 4096], P(('expert', 'dp'), 'half'), may hold values from -12 to 12
- expert_ids: int32 [4096, 8], P(('expert', 'dp')), may hold values from 0 to 15, as said below
- slot_ids: int32 [4096, 8], P(('expert', 'dp')), may hold values from 0 to 71, as said below
- gate_weights: float32 [4096, 8], P(('expert', 'dp')), may hold values from 0.03 to 0.4
- latent_down: bfloat16 [4096, 1024], P('half', 'dp'), may hold values from -0.09375 to 0.09375
- latent_up: bfloat16 [1024, 4096], P('dp', 'half'), may hold values from -0.1875 to 0.1875
- expert_gate: bfloat16 [16, 1024, 1536], P('expert', 'dp', 'half'), may hold values from -0.1875 to 0.1875
- expert_linear: bfloat16 [16, 1024, 1536], P('expert', 'dp', 'half'), may hold values from -0.1875 to 0.1875
- expert_out: bfloat16 [16, 1536, 1024], P('expert', 'half', 'dp'), may hold values from -0.15625 to 0.15625
Outputs:
- token_grad: bfloat16 [4096, 4096], P(('expert', 'dp'), 'half')
- gate_grad: bfloat16 [16, 1024, 1536], P('expert', 'dp', 'half')
- linear_grad: bfloat16 [16, 1024, 1536], P('expert', 'dp', 'half')
- out_grad: bfloat16 [16, 1536, 1024], P('expert', 'half', 'dp')
Inputs may be any that keep to these rules, and one draw needn't show every extreme that they name: `expert_ids`: each row names 8 different experts. In each aligned block of 128 rows (the rows of one device) no expert is named by more than 72 rows, and one expert is named by exactly 72 rows in every block. `slot_ids`: within one aligned block of 128 rows, the entries that name the same expert have different slots.
All inputs are finite; a program needn't handle non-finite values.
Results may differ from a plain program's by a relative error of at most 0.013.
Values may be sent and summed in bfloat16 or wider, within the bound.
No kernel may reach another device: no remote copies, remote signals or barrier semaphores. Data moves between devices by JAX's collectives and lax.ppermute only.
A program may use at most 128 MiB of HBM per device.

v0:
```python
import jax
import jax.numpy as jnp
from jax import lax
from jax.sharding import PartitionSpec as P


def on_device(
    tokens,
    cotangent,
    expert_ids,
    slot_ids,
    gate_weights,
    latent_down,
    latent_up,
    expert_gate,
    expert_linear,
    expert_out,
):
    row_count = tokens.shape[0]
    pick_count = expert_ids.shape[1]
    local_count = expert_gate.shape[0]
    group_count = lax.axis_size("expert")
    expert_count = group_count * local_count
    capacity = min(
        row_count, 2 * ((9 * row_count * pick_count + 16 * expert_count - 1) // (16 * expert_count))
    )
    down_full, up_full, gate_full, linear_full, output_full = (
        lax.all_gather(latent_down, "dp", axis=1, tiled=True),
        lax.all_gather(latent_up, "dp", axis=0, tiled=True),
        lax.all_gather(expert_gate, "dp", axis=1, tiled=True),
        lax.all_gather(expert_linear, "dp", axis=1, tiled=True),
        lax.all_gather(expert_out, "dp", axis=2, tiled=True),
    )
    latent_part = jnp.dot(tokens, down_full, preferred_element_type=jnp.float32)
    back_part = lax.dot_general(
        cotangent, up_full, (((1,), (1,)), ((), ())), preferred_element_type=jnp.float32
    )
    latent_sum, back_latent = lax.psum((latent_part, back_part), "half")
    latent = latent_sum.astype(jnp.bfloat16)
    width = latent.shape[1]
    flat_slot = (expert_ids * capacity + slot_ids).reshape(-1)
    slot_table = lax.broadcasted_iota(
        jnp.int32, (expert_count * capacity, row_count * pick_count), 0
    )
    matches = flat_slot[None, :] == slot_table
    choice_index = lax.broadcasted_iota(jnp.int32, matches.shape, 1)
    source = jnp.sum(jnp.where(matches, choice_index, 0), axis=1)
    filled = jnp.any(matches, axis=1)
    token_of = source // pick_count
    gate_of = gate_weights.reshape(-1)[source]
    send_latent = jnp.where(filled[:, None], latent[token_of], jnp.zeros((), jnp.bfloat16))
    send_back = jnp.where(filled[:, None], gate_of[:, None] * back_latent[token_of], 0.0).astype(
        jnp.bfloat16
    )
    send_latent = send_latent.reshape(group_count, local_count, capacity, width)
    send_back = send_back.reshape(group_count, local_count, capacity, width)
    rows_latent, rows_back = (
        lax.all_to_all(send_latent, "expert", split_axis=0, concat_axis=0, tiled=True),
        lax.all_to_all(send_back, "expert", split_axis=0, concat_axis=0, tiled=True),
    )
    pre_gate = jnp.einsum(
        "neci,eih->nech", rows_latent, gate_full, preferred_element_type=jnp.float32
    )
    pre_linear = jnp.einsum(
        "neci,eih->nech", rows_latent, linear_full, preferred_element_type=jnp.float32
    )
    grad_hidden = jnp.einsum(
        "necj,ehj->nech", rows_back, output_full, preferred_element_type=jnp.float32
    )
    logistic = jax.nn.sigmoid(pre_gate)
    hidden = (pre_gate * logistic * pre_linear).astype(jnp.bfloat16)
    gate_delta = (grad_hidden * pre_linear * logistic * (1.0 + pre_gate * (1.0 - logistic))).astype(
        jnp.bfloat16
    )
    linear_delta = (grad_hidden * pre_gate * logistic).astype(jnp.bfloat16)
    gate_part = jnp.einsum(
        "neci,nech->eih", rows_latent, gate_delta, preferred_element_type=jnp.float32
    )
    linear_part = jnp.einsum(
        "neci,nech->eih", rows_latent, linear_delta, preferred_element_type=jnp.float32
    )
    out_part = jnp.einsum("nech,necj->ehj", hidden, rows_back, preferred_element_type=jnp.float32)
    gate_share, linear_share, out_share = (
        lax.psum_scatter(
            gate_part.astype(jnp.bfloat16), "dp", scatter_dimension=1, tiled=True
        ).astype(jnp.float32),
        lax.psum_scatter(
            linear_part.astype(jnp.bfloat16), "dp", scatter_dimension=1, tiled=True
        ).astype(jnp.float32),
        lax.psum_scatter(
            out_part.astype(jnp.bfloat16), "dp", scatter_dimension=2, tiled=True
        ).astype(jnp.float32),
    )
    row_part = jnp.einsum(
        "nech,eih->neci", gate_delta, gate_full, preferred_element_type=jnp.float32
    )
    row_part = row_part + jnp.einsum(
        "nech,eih->neci", linear_delta, linear_full, preferred_element_type=jnp.float32
    )
    row_whole = lax.psum(row_part, "half").astype(jnp.bfloat16)
    returned = lax.all_to_all(row_whole, "expert", split_axis=0, concat_axis=0, tiled=True)
    position = expert_ids * capacity + slot_ids
    gathered = returned.reshape(expert_count * capacity, width)[position]
    latent_grad = jnp.sum(gathered.astype(jnp.float32), axis=1)
    token_grad = lax.dot_general(
        latent_grad.astype(jnp.bfloat16),
        down_full,
        (((1,), (1,)), ((), ())),
        preferred_element_type=jnp.float32,
    )
    return (
        token_grad.astype(jnp.bfloat16),
        gate_share.astype(jnp.bfloat16),
        linear_share.astype(jnp.bfloat16),
        out_share.astype(jnp.bfloat16),
    )


def solution(mesh):
    in_specs = (
        P(("expert", "dp"), "half"),
        P(("expert", "dp"), "half"),
        P(("expert", "dp"), None),
        P(("expert", "dp"), None),
        P(("expert", "dp"), None),
        P("half", "dp"),
        P("dp", "half"),
        P("expert", "dp", "half"),
        P("expert", "dp", "half"),
        P("expert", "half", "dp"),
    )
    out_specs = (
        P(("expert", "dp"), "half"),
        P("expert", "dp", "half"),
        P("expert", "dp", "half"),
        P("expert", "half", "dp"),
    )
    return jax.shard_map(
        on_device, mesh=mesh, in_specs=in_specs, out_specs=out_specs, check_vma=False
    )
```

profile of v0, /device:TPU:0, one launch (start us, length us, event | category | flops | bytes accessed | tf_op | source)
XLA Modules:
  0.0 298.2 jit_solution(3068094195249041496)
XLA Ops:
  7.2 0.0 copy-start
  7.2 0.0 all-gather.6.cloned.1.call-start
  7.2 0.0 copy-start.4
  7.2 0.0 copy-start.5
  7.2 0.0 copy-start.3
  7.3 0.7 all-gather.6.cloned.1.call-update
  7.9 0.0 all-gather.10.cloned.1.call-start
  8.0 0.7 all-gather.10.cloned.1.call-update
  8.7 0.0 copy-done.4
  8.7 0.0 copy-done.5
  8.7 0.1 copy.23
  8.8 0.1 eq.10
  8.9 0.6 fusion.10
  9.5 0.1 broadcast_in_dim.37
  9.6 0.0 copy-done.3
  9.6 0.1 copy.24
  9.7 0.1 reshape.178
  9.8 0.6 select_reduce_fusion
  10.4 0.1 fusion.47
  10.4 4.6 %gather_fusion = f32[1152]{0:T(1024)S(1)} fusion(f32[1024]{0:T(1024)S(1)} %reshape.178, s32[2048]{0:T(1024)S(1)} %pad_clamp_fusion.1), kind=kCustom, calls=%fused_computation | custom fusion | bytes 13824 | tf_op jit(solution)/shard_map/gather | solution.py:50
  15.0 0.1 mul.46
  15.1 17.0 %all-gather.6.cloned.1.call-done = bf16[1024,4096]{1,0:T(8,128)(2,1)} async-done(((bf16[512,4096]{1,0:T(8,128)(2,1)}), bf16[1024,4096]{1,0:T(8,128)(2,1)}) %all-gather.6.cloned.1.call-update) | async-done | bytes 8388624 | tf_op jit(solution)/shard_map/all_gather | solution.py:29
  32.1 6.3 %fusion.50 = f32[128,1024]{1,0:T(8,128)S(1)} fusion(bf16[128,4096]{1,0:T(8,128)(2,1)S(1)} %copy-done, bf16[1024,4096]{1,0:T(8,128)(2,1)} %all-gather.6.cloned.1.call-done), kind=kOutput, calls=%fused_computation.71 | convolution fusion | flops 1073741824 | bytes 9961472 | tf_op jit(solution)/shard_map/dot_general | solution.py:35
  38.4 5.1 %gather_fusion.1 = f32[1152,1024]{1,0:T(8,128)} fusion(f32[128,1024]{1,0:T(8,128)S(1)} %fusion.50, s32[2048]{0:T(1024)S(1)} %pad_clamp_fusion), kind=kCustom, calls=%fused_computation.1 | custom fusion | bytes 9441792 | tf_op jit(solution)/shard_map/gather | solution.py:52
  43.5 4.6 %select_convert_fusion = bf16[16,1,72,1024]{3,2,1,0:T(8,128)(2,1)} fusion(f32[16,1,72,1024]{3,2,1,0:T(8,128)} %bitcast.162, f32[16,72]{1,0:T(8,128)S(1)} %mul.46, pred[16,72]{1,0:T(8,128)(4,1)S(1)} %broadcast_in_dim.37), kind=kLoop, calls=%fused_computation.25 | loop fusion | flops 3538944 | bytes 7083648 | tf_op jit(solution)/shard_map/convert_element_type | solution.py:52
  48.1 7.0 %all-to-all-start = ((bf16[16,1,72,1024]{3,2,1,0:T(8,128)(2,1)}), bf16[16,1,72,1024]{3,2,1,0:T(8,128)(2,1)}, u32[]{:S(2)}, u32[]{:S(2)}) async-start(bf16[16,1,72,1024]{3,2,1,0:T(8,128)(2,1)} %select_convert_fusion), calls=%async_computation | async-start | bytes 4718592 | tf_op jit(solution)/shard_map/all_to_all | solution.py:59
  55.0 0.0 all-gather.8.cloned.1.call-start
  55.1 0.7 all-gather.8.cloned.1.call-update
  55.8 0.0 all-gather.14.cloned.1.call-start
  55.8 0.5 all-gather.14.cloned.1.call-update
  56.4 0.0 all-gather.10.cloned.1.call-done
  56.4 0.0 copy-done.2
  56.4 4.6 %convolution_convert_fusion.1 = bf16[128,1024]{1,0:T(8,128)(2,1)S(1)} fusion(bf16[128,4096]{1,0:T(8,128)(2,1)S(1)} %copy-done.2, bf16[4096,1024]{1,0:T(8,128)(2,1)} %all-gather.10.cloned.1.call-done), kind=kOutput, calls=%fused_computation.56 | convolution fusion | flops 1073872896 | bytes 9699328 | tf_op jit(solution)/shard_map/dot_general | solution.py:34
  61.0 4.4 %gather_fusion.2 = bf16[1152,1024]{1,0:T(8,128)(2,1)S(1)} fusion(bf16[128,1024]{1,0:T(8,128)(2,1)S(1)} %convolution_convert_fusion.1, s32[2048]{0:T(1024)S(1)} %pad_clamp_fusion), kind=kCustom, calls=%fused_computation.2 | custom fusion | bytes 4723200 | tf_op jit(solution)/shard_map/gather | solution.py:51
  65.4 1.6 broadcast_select_fusion
  67.1 35.7 %all-to-all-done = bf16[16,1,72,1024]{3,2,1,0:T(8,128)(2,1)} async-done(((bf16[16,1,72,1024]{3,2,1,0:T(8,128)(2,1)}), bf16[16,1,72,1024]{3,2,1,0:T(8,128)(2,1)}, u32[]{:S(2)}, u32[]{:S(2)}) %all-to-all-start) | async-done | bytes 2359328 | tf_op jit(solution)/shard_map/all_to_all | solution.py:59
  102.8 11.8 %all-to-all-start.1 = ((bf16[16,1,72,1024]{3,2,1,0:T(8,128)(2,1)}), bf16[16,1,72,1024]{3,2,1,0:T(8,128)(2,1)S(1)}, u32[]{:S(2)}, u32[]{:S(2)}) async-start(bf16[16,1,72,1024]{3,2,1,0:T(8,128)(2,1)} %broadcast_select_fusion), calls=%async_computation.1 | async-start | bytes 4718592 | tf_op jit(solution)/shard_map/all_to_all | solution.py:58
  114.6 0.0 all-gather.12.cloned.1.call-start
  114.6 0.5 all-gather.12.cloned.1.call-update
  115.2 0.2 reduce-scatter.8.cloned.1.call-start
  115.4 0.0 all-gather.8.cloned.1.call-done
  115.4 9.4 %fusion.34 = f32[16,72,1536]{2,1,0:T(8,128)} fusion(bf16[1,1536,1024]{2,1,0:T(8,128)(2,1)} %all-gather.8.cloned.1.call-done, bf16[16,1,72,1024]{3,2,1,0:T(8,128)(2,1)} %all-to-all-done), kind=kOutput, calls=%fused_computation.45 | convolution fusion | flops 3623878656 | bytes 12582912 | tf_op jit(solution)/shard_map/necj,ehj->nech/dot_general | solution.py:67
  124.8 36.8 %all-to-all-done.1 = bf16[16,1,72,1024]{3,2,1,0:T(8,128)(2,1)S(1)} async-done(((bf16[16,1,72,1024]{3,2,1,0:T(8,128)(2,1)}), bf16[16,1,72,1024]{3,2,1,0:T(8,128)(2,1)S(1)}, u32[]{:S(2)}, u32[]{:S(2)}) %all-to-all-start.1) | async-done | bytes 2359328 | tf_op jit(solution)/shard_map/all_to_all | solution.py:58
  161.7 7.7 %fusion.29 = f32[16,72,1536]{2,1,0:T(8,128)} fusion(bf16[1,1024,1536]{2,1,0:T(8,128)(2,1)} %all-gather.14.cloned.1.call-done, bf16[16,1,72,1024]{3,2,1,0:T(8,128)(2,1)S(1)} %all-to-all-done.1), kind=kOutput, calls=%fused_computation.40 | convolution fusion | flops 3623878656 | bytes 12582912 | tf_op jit(solution)/shard_map/neci,eih->nech/dot_general | solution.py:61
  169.4 12.3 %fusion.2 = (bf16[16,1,72,1536]{3,2,0,1:T(8,128)(2,1)}, bf16[16,1,72,1536]{3,2,0,1:T(8,128)(2,1)}, f32[16,72,1536]{2,1,0:T(8,128)S(1)}) fusion(f32[16,72,1536]{2,1,0:T(8,128)} %fusion.34, f32[16,72,1536]{2,1,0:T(8,128)} %fusion.29, bf16[1,1024,1536]{2,1,0:T(8,128)(2,1)} %all-gather.12.cloned.1.call-done, bf16[16,1,72,1024]{3,2,1,0:T(8,128)(2,1)S(1)} %all-to-all-done.1), kind=kOutput, calls=%fused_computation.8 | convolution fusion | flops 3646881792 | bytes 33816576 | tf_op jit(solution)/shard_map/neci,eih->nech/dot_general | solution.py:64
  181.7 7.7 %fusion.25 = bf16[1,1536,1024]{2,1,0:T(8,128)(2,1)} fusion(f32[16,72,1536]{2,1,0:T(8,128)S(1)} %get-tuple-element.10, f32[16,72,1536]{2,1,0:T(8,128)S(1)} %copy-done.7, bf16[16,1,72,1024]{3,2,1,0:T(8,128)(2,1)} %all-to-all-done), kind=kOutput, calls=%fused_computation.38 | convolution fusion | flops 3636068352 | bytes 19660800 | tf_op jit(solution)/shard_map/nech,necj->ehj/dot_general | solution.py:82
  189.5 0.0 reduce-scatter.8.cloned.1.call-update
  189.5 0.0 reduce-scatter.6.cloned.1.call-start
  189.5 7.7 %fusion.22 = bf16[1,1024,1536]{2,1,0:T(8,128)(2,1)} fusion(bf16[16,1,72,1536]{3,2,0,1:T(8,128)(2,1)} %get-tuple-element.9, bf16[16,1,72,1024]{3,2,1,0:T(8,128)(2,1)S(1)} %all-to-all-done.1), kind=kOutput, calls=%fused_computation.37 | convolution fusion | flops 3625451520 | bytes 9043968 | tf_op jit(solution)/shard_map/neci,nech->eih/dot_general | solution.py:79
  197.2 0.0 reduce-scatter.6.cloned.1.call-update
  197.2 0.3 reduce-scatter.4.cloned.1.call-start
  197.5 7.7 %fusion.19 = bf16[1,1024,1536]{2,1,0:T(8,128)(2,1)} fusion(bf16[16,1,72,1536]{3,2,0,1:T(8,128)(2,1)} %get-tuple-element.8, bf16[16,1,72,1024]{3,2,1,0:T(8,128)(2,1)S(1)} %all-to-all-done.1), kind=kOutput, calls=%fused_computation.36 | convolution fusion | flops 3625451520 | bytes 9043968 | tf_op jit(solution)/shard_map/neci,nech->eih/dot_general | solution.py:76
  205.2 0.0 reduce-scatter.4.cloned.1.call-update
  205.2 0.0 copy-start.6
  205.2 0.0 copy-start.8
  205.2 7.0 %fusion.13 = f32[16,72,1024]{2,1,0:T(8,128)S(1)} fusion(bf16[16,1,72,1536]{3,2,0,1:T(8,128)(2,1)} %get-tuple-element.9, bf16[1,1024,1536]{2,1,0:T(8,128)(2,1)} %all-gather.12.cloned.1.call-done), kind=kOutput, calls=%fused_computation.31 | convolution fusion | flops 3623878656 | bytes 11403264 | tf_op jit(solution)/shard_map/nech,eih->neci/dot_general | solution.py:97
  212.3 5.4 %fusion.36 = bf16[16,1,72,1024]{3,2,1,0:T(8,128)(2,1)} fusion(f32[16,72,1024]{2,1,0:T(8,128)S(1)} %fusion.13, bf16[1,1024,1536]{2,1,0:T(8,128)(2,1)S(1)} %copy-done.6, bf16[16,1,72,1536]{3,2,0,1:T(8,128)(2,1)S(1)} %copy-done.8), kind=kOutput, calls=%fused_computation.47 | convolution fusion | flops 3626237952 | bytes 13762560 | tf_op jit(solution)/shard_map/nech,eih->neci/dot_general | solution.py:94
  217.7 11.0 %all-to-all-start.2 = ((bf16[16,1,72,1024]{3,2,1,0:T(8,128)(2,1)}), bf16[16,1,72,1024]{3,2,1,0:T(8,128)(2,1)S(1)}, u32[]{:S(2)}, u32[]{:S(2)}) async-start(bf16[16,1,72,1024]{3,2,1,0:T(8,128)(2,1)} %fusion.36), calls=%async_computation.2 | async-start | bytes 4718592 | tf_op jit(solution)/shard_map/all_to_all | solution.py:101
  228.7 0.1 copy.28
  228.8 0.1 reshape.214
  228.9 46.7 %all-to-all-done.2 = bf16[16,1,72,1024]{3,2,1,0:T(8,128)(2,1)S(1)} async-done(((bf16[16,1,72,1024]{3,2,1,0:T(8,128)(2,1)}), bf16[16,1,72,1024]{3,2,1,0:T(8,128)(2,1)S(1)}, u32[]{:S(2)}, u32[]{:S(2)}) %all-to-all-start.2) | async-done | bytes 2359328 | tf_op jit(solution)/shard_map/all_to_all | solution.py:101
  275.6 5.4 %gather_fusion.3 = bf16[1024,1024]{1,0:T(8,128)(2,1)} fusion(bf16[1152,1024]{1,0:T(8,128)(2,1)S(1)} %bitcast.161, s32[1024]{0:T(1024)S(1)} %broadcast_clamp_fusion), kind=kCustom, calls=%fused_computation.3 | custom fusion | bytes 4198400 | tf_op jit(solution)/shard_map/gather | solution.py:103
  281.0 3.1 %bitcast_reduce_fusion = bf16[128,1024]{1,0:T(8,128)(2,1)S(1)} fusion(bf16[1024,1024]{1,0:T(8,128)(2,1)} %gather_fusion.3), kind=kLoop, calls=%fused_computation.55 | loop fusion | flops 917504 | bytes 2359296 | tf_op jit(solution)/shard_map/reduce_sum | solution.py:104
  284.1 7.2 %convolution_convert_fusion = bf16[128,4096]{1,0:T(8,128)(2,1)} fusion(bf16[128,1024]{1,0:T(8,128)(2,1)S(1)} %bitcast_reduce_fusion, bf16[4096,1024]{1,0:T(8,128)(2,1)} %all-gather.10.cloned.1.call-done), kind=kOutput, calls=%fused_computation.23 | convolution fusion | flops 1074266112 | bytes 9699328 | tf_op jit(solution)/shard_map/dot_general | solution.py:105
  (17 shorter events, 0.1 us)
Async XLA Ops:
  7.2 25.0 %copy-start = (bf16[128,4096]{1,0:T(8,128)(2,1)S(1)}, bf16[128,4096]{1,0:T(8,128)(2,1)}, u32[]{:S(2)}) copy-start(bf16[128,4096]{1,0:T(8,128)(2,1)} %param.11) | copy-start | bytes 3145732
  7.2 25.0 %all-gather.6.cloned.1.call-start = ((), (), s32[]{:S(2)}) async-start(), calls=%async_computation.6 | async-start | bytes 12582912 | tf_op jit(solution)/shard_map/all_gather | solution.py:29
  7.2 1.4 copy-start.4
  7.2 1.4 copy-start.5
  7.2 2.4 copy-start.3
  7.9 48.5 %all-gather.10.cloned.1.call-start = ((), (), s32[]{:S(2)}) async-start(), calls=%async_computation.8 | async-start | bytes 12582912 | tf_op jit(solution)/shard_map/all_gather | solution.py:28
  48.1 8.3 %copy-start.2 = (bf16[128,4096]{1,0:T(8,128)(2,1)S(1)}, bf16[128,4096]{1,0:T(8,128)(2,1)}, u32[]{:S(2)}) copy-start(bf16[128,4096]{1,0:T(8,128)(2,1)} %param.10) | copy-start | bytes 3145732
  48.1 54.7 %all-to-all-start = ((bf16[16,1,72,1024]{3,2,1,0:T(8,128)(2,1)}), bf16[16,1,72,1024]{3,2,1,0:T(8,128)(2,1)}, u32[]{:S(2)}, u32[]{:S(2)}) async-start(bf16[16,1,72,1024]{3,2,1,0:T(8,128)(2,1)} %select_convert_fusion), calls=%async_computation | async-start | bytes 4718592 | tf_op jit(solution)/shard_map/all_to_all | solution.py:59
  55.0 60.4 %all-gather.8.cloned.1.call-start = ((), (), s32[]{:S(2)}) async-start(), calls=%async_computation.7 | async-start | bytes 4718592 | tf_op jit(solution)/shard_map/all_gather | solution.py:32
  55.8 69.0 %all-gather.14.cloned.1.call-start = ((), (), s32[]{:S(2)}) async-start(), calls=%async_computation.10 | async-start | bytes 4718592 | tf_op jit(solution)/shard_map/all_gather | solution.py:30
  102.8 58.9 %all-to-all-start.1 = ((bf16[16,1,72,1024]{3,2,1,0:T(8,128)(2,1)}), bf16[16,1,72,1024]{3,2,1,0:T(8,128)(2,1)S(1)}, u32[]{:S(2)}, u32[]{:S(2)}) async-start(bf16[16,1,72,1024]{3,2,1,0:T(8,128)(2,1)} %broadcast_select_fusion), calls=%async_computation.1 | async-start | bytes 4718592 | tf_op jit(solution)/shard_map/all_to_all | solution.py:58
  114.6 54.8 %all-gather.12.cloned.1.call-start = ((), (), s32[]{:S(2)}) async-start(), calls=%async_computation.9 | async-start | bytes 4718592 | tf_op jit(solution)/shard_map/all_gather | solution.py:31
  115.2 176.2 %reduce-scatter.8.cloned.1.call-start = ((), (), s32[]{:S(2)}) async-start(), calls=%async_computation.13 | async-start | bytes 4718592 | tf_op jit(solution)/shard_map/reduce_scatter | solution.py:90
  169.4 12.3 %copy-start.7 = (f32[16,72,1536]{2,1,0:T(8,128)S(1)}, f32[16,72,1536]{2,1,0:T(8,128)}, u32[]{:S(2)}) copy-start(f32[16,72,1536]{2,1,0:T(8,128)} %fusion.29) | copy-start | bytes 21233668
  189.5 101.9 %reduce-scatter.6.cloned.1.call-start = ((), (), s32[]{:S(2)}) async-start(), calls=%async_computation.12 | async-start | bytes 4718592 | tf_op jit(solution)/shard_map/reduce_scatter | solution.py:87
  197.2 94.1 %reduce-scatter.4.cloned.1.call-start = ((), (), s32[]{:S(2)}) async-start(), calls=%async_computation.11 | async-start | bytes 4718592 | tf_op jit(solution)/shard_map/reduce_scatter | solution.py:84
  205.2 7.1 %copy-start.6 = (bf16[1,1024,1536]{2,1,0:T(8,128)(2,1)S(1)}, bf16[1,1024,1536]{2,1,0:T(8,128)(2,1)}, u32[]{:S(2)}) copy-start(bf16[1,1024,1536]{2,1,0:T(8,128)(2,1)} %all-gather.14.cloned.1.call-done) | copy-start | bytes 9437188
  205.2 7.1 %copy-start.8 = (bf16[16,1,72,1536]{3,2,0,1:T(8,128)(2,1)S(1)}, bf16[16,1,72,1536]{3,2,0,1:T(8,128)(2,1)}, u32[]{:S(2)}) copy-start(bf16[16,1,72,1536]{3,2,0,1:T(8,128)(2,1)} %get-tuple-element.8) | copy-start | bytes 10616836
  217.7 57.9 %all-to-all-start.2 = ((bf16[16,1,72,1024]{3,2,1,0:T(8,128)(2,1)}), bf16[16,1,72,1024]{3,2,1,0:T(8,128)(2,1)S(1)}, u32[]{:S(2)}, u32[]{:S(2)}) async-start(bf16[16,1,72,1024]{3,2,1,0:T(8,128)(2,1)} %fusion.36), calls=%async_computation.2 | async-start | bytes 4718592 | tf_op jit(solution)/shard_map/all_to_all | solution.py:101
  281.0 10.4 %copy-start.1 = (bf16[128,4096]{1,0:T(8,128)(2,1)S(1)}, bf16[128,4096]{1,0:T(8,128)(2,1)}, u32[]{:S(2)}) copy-start(bf16[128,4096]{1,0:T(8,128)(2,1)} %param.11) | copy-start | bytes 3145732
Sparse Core Ops, SparseCore 0:
  9.6 22.5 all-gather.5
  33.7 21.0 all-gather.9
  57.4 13.3 all-gather.7
  72.2 13.2 all-gather.13
  116.6 13.4 all-gather.11
  189.6 16.0 reduce-scatter.7
  208.6 12.0 reduce-scatter.5
  223.5 12.0 reduce-scatter.3
where the time goes:
time: 304 us; the launch traced here: 298 us
  waiting for transfers between devices  139 us (46%)
  matrix products  83.1 us (27%)
  starting transfers between devices  30.5 us (10%)
  local copies, waits for them, and re-layouts  20.2 us (7%)
  between operations  14.4 us (5%)
  other arithmetic  10.6 us (3%)
    all_to_all x1, waiting for transfers between devices, on_device(): lax.all_to_all(row_whole, 'expert', split_axis=0, concat_axis=0, tiled=True)  46.7 us
    all_to_all x1, waiting for transfers between devices, on_device(): lax.all_to_all(send_latent, 'expert', split_axis=0, concat_axis=0, tiled=...  36.8 us
    all_to_all x1, waiting for transfers between devices, on_device(): lax.all_to_all(send_back, 'expert', split_axis=0, concat_axis=0, tiled=True)  35.7 us
    all_gather x1, waiting for transfers between devices, on_device(): lax.all_gather(latent_up, 'dp', axis=0, tiled=True)  17 us
    dot_general x1, matrix products, on_device(): jnp.einsum('neci,eih->nech', rows_latent, linear_full, preferred_element_...  12.3 us
    all_to_all x1, starting transfers between devices, on_device(): lax.all_to_all(send_latent, 'expert', split_axis=0, concat_axis=0, tiled=...  11.8 us
    all_to_all x1, starting transfers between devices, on_device(): lax.all_to_all(row_whole, 'expert', split_axis=0, concat_axis=0, tiled=True)  11 us
    dot_general x1, matrix products, on_device(): jnp.einsum('necj,ehj->nech', rows_back, output_full, preferred_element_ty...  9.41 us
  transfers between devices with their start and end apart: 11, of which 4 were waited for; matrix products, arithmetic and copies ran while one was open for 31% of the time, Pallas kernels for 0%

commit v1 on v0

v1 whole, which is shorter than its diff:
```python
import functools

import jax
import jax.numpy as jnp
from jax import lax
from jax.experimental import pallas as pl
from jax.experimental.pallas import tpu as pltpu
from jax.sharding import PartitionSpec as P

BF = jnp.bfloat16
F32 = jnp.float32
PLANES = 4
VMEM_LIMIT = 56 * 1024 * 1024
ROWS = (((0,), (0,)), ((), ()))
LAST = (((1,), (1,)), ((), ()))


def pad16(n):
    return (n + 15) // 16 * 16


def params():
    return pltpu.CompilerParams(vmem_limit_bytes=VMEM_LIMIT)


def cost(flops, moved):
    return pl.CostEstimate(flops=int(flops), bytes_accessed=int(moved), transcendentals=0)


def whole(shape):
    return pl.BlockSpec(shape, lambda *_: (0,) * len(shape))


def one_hot(meta_ref, picks, inner, cap, padded, weighted):
    me = lax.axis_index("expert")
    place = lax.rem(me, inner)
    first = me - place
    tokens = meta_ref.shape[1]
    slot = lax.broadcasted_iota(jnp.int32, (padded, tokens), 0)
    targets = []
    for k in range(inner):
        base = (first + lax.bitwise_xor(place, k)) * cap
        targets.append(jnp.where(slot < cap, slot + base, -1))
    target = jnp.concatenate(targets, axis=0).astype(F32)
    mark = jnp.zeros(target.shape, F32)
    weight = jnp.zeros(target.shape, F32)
    for j in range(picks):
        equal = target == meta_ref[j : j + 1, :]
        mark = jnp.where(equal, 1.0, mark)
        if weighted:
            weight = jnp.where(equal, meta_ref[picks + j : picks + j + 1, :], weight)
    return mark, (jnp.sum(weight, axis=1, keepdims=True) if weighted else None)


def select_body(picks, inner, cap, padded, weighted, meta_ref, block_ref, *piece_refs):
    mark, weight = one_hot(meta_ref, picks, inner, cap, padded, weighted)
    rows = jnp.dot(mark.astype(BF), block_ref[...], preferred_element_type=F32)
    if weighted:
        rows = rows * weight
    for k in range(inner):
        piece_refs[k][...] = rows[k * padded : k * padded + cap, :].astype(BF)


def select(meta, block, inner, cap, weighted):
    picks = meta.shape[0] // 2
    padded = pad16(cap)
    tokens, width = block.shape
    return pl.pallas_call(
        functools.partial(select_body, picks, inner, cap, padded, weighted),
        out_shape=[jax.ShapeDtypeStruct((cap, width), BF)] * inner,
        compiler_params=params(),
        cost_estimate=cost(2 * inner * padded * tokens * width, 4 * tokens * width),
        name="select_back" if weighted else "select_latent",
    )(meta, block)


def assemble(piece_refs, out_ref, cap, padded):
    for i, ref in enumerate(piece_refs):
        if padded > cap:
            out_ref[(i + 1) * padded - 16 : (i + 1) * padded, :] = jnp.zeros(
                (16, out_ref.shape[1]), out_ref.dtype
            )
        out_ref[i * padded : i * padded + cap, :] = ref[...]


def expand_body(picks, inner, cap, padded, meta_ref, *refs):
    piece_refs, out_ref, held = refs[:inner], refs[inner], refs[inner + 1]
    assemble(piece_refs, held, cap, padded)
    mark, _ = one_hot(meta_ref, picks, inner, cap, padded, False)
    out_ref[...] = lax.dot_general(
        mark.astype(BF), held[...], ROWS, preferred_element_type=F32
    ).astype(out_ref.dtype)


def expand(meta, pieces, dtype):
    picks, tokens = meta.shape[0] // 2, meta.shape[1]
    inner = len(pieces)
    cap, width = pieces[0].shape
    padded = pad16(cap)
    return pl.pallas_call(
        functools.partial(expand_body, picks, inner, cap, padded),
        out_shape=jax.ShapeDtypeStruct((tokens, width), dtype),
        scratch_shapes=[pltpu.VMEM((inner * padded, width), BF)],
        compiler_params=params(),
        cost_estimate=cost(2 * inner * padded * tokens * width, 4 * tokens * width),
        name="expand_rows",
    )(meta, *pieces)


def forward_body(count, cap, padded, *refs):
    piece_refs = refs[:count]
    gate_m, gate_o, linear_m, linear_o, x_ref, pre_gate_ref, pre_linear_ref = refs[count:]

    @pl.when(pl.program_id(0) == 0)
    def _():
        assemble(piece_refs, x_ref, cap, padded)

    half = x_ref.shape[1] // 2
    mine, other = x_ref[:, :half], x_ref[:, half:]
    for m_ref, o_ref, out in ((gate_m, gate_o, pre_gate_ref), (linear_m, linear_o, pre_linear_ref)):
        out[...] = jnp.dot(mine, m_ref[...], preferred_element_type=F32) + jnp.dot(
            other, o_ref[...], preferred_element_type=F32
        )


def forward(pieces, weights, tile):
    count = len(pieces)
    cap, width = pieces[0].shape
    padded = pad16(cap)
    rows = count * padded
    hidden = weights[0].shape[1]
    column = lambda j: (0, j)
    return pl.pallas_call(
        functools.partial(forward_body, count, cap, padded),
        grid=(hidden // tile,),
        in_specs=[whole((cap, width))] * count + [pl.BlockSpec((width // 2, tile), column)] * 4,
        out_specs=[whole((rows, width))] + [pl.BlockSpec((rows, tile), column)] * 2,
        out_shape=[jax.ShapeDtypeStruct((rows, width), BF)]
        + [jax.ShapeDtypeStruct((rows, hidden), F32)] * 2,
        compiler_params=params(),
        cost_estimate=cost(4 * rows * width * hidden, 8 * rows * hidden + 4 * width * hidden),
        name="forward_rows",
    )(*pieces, *weights)


def backward_body(count, cap, padded, *refs):
    piece_refs = refs[:count]
    (pre_gate_ref, pre_linear_ref, out_m, out_o, gate_m, gate_o, linear_m, linear_o) = refs[
        count : count + 8
    ]
    b_ref, gate_delta_ref, linear_delta_ref, hidden_ref = refs[count + 8 : count + 12]
    row_refs = refs[count + 12 : 2 * count + 12]
    total = refs[2 * count + 12]
    step = pl.program_id(0)

    @pl.when(step == 0)
    def _():
        assemble(piece_refs, b_ref, cap, padded)

    half = b_ref.shape[1] // 2
    grad_hidden = lax.dot_general(
        b_ref[:, :half], out_m[...], LAST, preferred_element_type=F32
    ) + lax.dot_general(b_ref[:, half:], out_o[...], LAST, preferred_element_type=F32)
    pre_gate, pre_linear = pre_gate_ref[...], pre_linear_ref[...]
    logistic = jax.nn.sigmoid(pre_gate)
    scaled = pre_gate * logistic
    hidden_ref[...] = (scaled * pre_linear).astype(BF)
    linear_delta = (grad_hidden * scaled).astype(BF)
    gate_delta = (
        grad_hidden * pre_linear * logistic * (1.0 + pre_gate * (1.0 - logistic))
    ).astype(BF)
    gate_delta_ref[...] = gate_delta
    linear_delta_ref[...] = linear_delta
    parts = []
    for gate, linear in ((gate_m, linear_m), (gate_o, linear_o)):
        parts.append(
            lax.dot_general(gate_delta, gate[...], LAST, preferred_element_type=F32)
            + lax.dot_general(linear_delta, linear[...], LAST, preferred_element_type=F32)
        )

    @pl.when(step == 0)
    def _():
        total[:, :half] = parts[0]
        total[:, half:] = parts[1]

    @pl.when(step > 0)
    def _():
        total[:, :half] += parts[0]
        total[:, half:] += parts[1]

    @pl.when(step == pl.num_programs(0) - 1)
    def _():
        for i, ref in enumerate(row_refs):
            ref[...] = total[i * padded : i * padded + cap, :].astype(BF)


def backward(pieces, pre_gate, pre_linear, out_weights, weights, tile):
    count = len(pieces)
    cap, width = pieces[0].shape
    padded = pad16(cap)
    rows = count * padded
    hidden = pre_gate.shape[1]
    column = lambda j: (0, j)
    tiles = pl.BlockSpec((rows, tile), column)
    results = pl.pallas_call(
        functools.partial(backward_body, count, cap, padded),
        grid=(hidden // tile,),
        in_specs=[whole((cap, width))] * count
        + [tiles] * 2
        + [pl.BlockSpec((tile, width // 2), lambda j: (j, 0))] * 2
        + [pl.BlockSpec((width // 2, tile), column)] * 4,
        out_specs=[whole((rows, width))] + [tiles] * 3 + [whole((cap, width))] * count,
        out_shape=[jax.ShapeDtypeStruct((rows, width), BF)]
        + [jax.ShapeDtypeStruct((rows, hidden), BF)] * 3
        + [jax.ShapeDtypeStruct((cap, width), BF)] * count,
        scratch_shapes=[pltpu.VMEM((rows, width), F32)],
        compiler_params=params(),
        cost_estimate=cost(6 * rows * width * hidden, 14 * rows * hidden + 6 * width * hidden),
        name="backward_rows",
    )(*pieces, pre_gate, pre_linear, *out_weights, *weights)
    return results[:4], results[4:]


def weight_body(groups, add, *refs):
    ins = refs[: 5 * groups]
    at = 5 * groups
    received = refs[at : at + 3] if add else ()
    at += 3 if add else 0
    outs = refs[at : at + 3]
    totals = [None, None, None]
    for g in range(groups):
        x_ref, b_ref, gate_delta_ref, linear_delta_ref, hidden_ref = ins[5 * g : 5 * g + 5]
        for i, (a, b) in enumerate(
            ((x_ref, gate_delta_ref), (x_ref, linear_delta_ref), (hidden_ref, b_ref))
        ):
            term = lax.dot_general(a[...], b[...], ROWS, preferred_element_type=F32)
            totals[i] = term if totals[i] is None else totals[i] + term
    for i in range(3):
        if add:
            totals[i] = totals[i] + received[i][...].astype(F32)
        outs[i][...] = totals[i].astype(BF)


def weight_grads(groups, column, received, tile):
    hidden = groups[0][2].shape[1]
    width = groups[0][0].shape[1]
    in_specs, operands, total_rows = [], [], 0
    for x, b, gate_delta, linear_delta, hid in groups:
        rows = x.shape[0]
        total_rows += rows
        side = pl.BlockSpec((rows, width // 2), lambda j: (0, column))
        tiles = pl.BlockSpec((rows, tile), lambda j: (0, j))
        in_specs += [side, side, tiles, tiles, tiles]
        operands += [x, b, gate_delta, linear_delta, hid]
    wide = pl.BlockSpec((width // 2, tile), lambda j: (0, j))
    tall = pl.BlockSpec((tile, width // 2), lambda j: (j, 0))
    if received:
        in_specs += [wide, wide, tall]
        operands += list(received)
    return pl.pallas_call(
        functools.partial(weight_body, len(groups), bool(received)),
        grid=(hidden // tile,),
        in_specs=in_specs,
        out_specs=[wide, wide, tall],
        out_shape=[jax.ShapeDtypeStruct((width // 2, hidden), BF)] * 2
        + [jax.ShapeDtypeStruct((hidden, width // 2), BF)],
        compiler_params=params(),
        cost_estimate=cost(
            3 * total_rows * width * hidden, 6 * total_rows * hidden + 3 * width * hidden
        ),
        name="weight_grads",
    )(*operands)


def on_device(
    tokens,
    cotangent,
    expert_ids,
    slot_ids,
    gate_weights,
    latent_down,
    latent_up,
    expert_gate,
    expert_linear,
    expert_out,
):
    row_count = tokens.shape[0]
    pick_count = expert_ids.shape[1]
    group_count = lax.axis_size("expert")
    halves = lax.axis_size("half")
    expert_count = group_count * expert_gate.shape[0]
    capacity = min(
        row_count, 2 * ((9 * row_count * pick_count + 16 * expert_count - 1) // (16 * expert_count))
    )
    inner = group_count // PLANES
    tile = 256

    def swap(a):
        return lax.ppermute(a, "dp", [(0, 1), (1, 0)])

    def along(a, shift):
        return lax.ppermute(
            a,
            "expert",
            [
                (z * inner + p, (z + shift) % PLANES * inner + p)
                for z in range(PLANES)
                for p in range(inner)
            ],
        )

    def across(a, k):
        return lax.ppermute(a, "expert", [(i, i ^ k) for i in range(group_count)])

    def join(a):
        return lax.psum(a, "half") if halves > 1 else a

    position = (expert_ids * capacity + slot_ids).astype(F32)
    meta = jnp.concatenate([position, gate_weights], axis=1).T
    metas = [meta] + [along(meta, c) for c in range(1, PLANES)]

    def project(mine, weight, dims):
        def dot(a):
            return join(lax.dot_general(a, weight, dims, preferred_element_type=F32)).astype(BF)

        own = dot(mine)
        return jnp.concatenate([own, swap(dot(swap(mine)))], axis=1)

    latent = project(tokens, latent_down, (((1,), (0,)), ((), ())))
    back = project(cotangent, latent_up, LAST)

    gate, linear, out = expert_gate[0], expert_linear[0], expert_out[0]
    gate_pair, linear_pair, out_pair = (gate, swap(gate)), (linear, swap(linear)), (out, swap(out))
    down_pair = (latent_down, swap(latent_down))

    def spread(block, order, weighted):
        blocks = {0: block}
        for c in order:
            if c:
                blocks[c] = along(block, c)
        pieces = {}
        for c in order:
            parts = select(metas[c], blocks[c], inner, capacity, weighted)
            pieces[c] = [parts[0]] + [across(parts[k], k) for k in range(1, inner)]
        return pieces

    latent_pieces = spread(latent, (0, 1, 3, 2), False)
    back_pieces = spread(back, (2, 3, 0, 1), True)
    groups, partial = [], {}
    for chunks in ((2, 3), (0, 1)):
        x, pre_gate, pre_linear = forward(
            [a for c in chunks for a in latent_pieces[c]], (*gate_pair, *linear_pair), tile
        )
        (b, gate_delta, linear_delta, hid), rows = backward(
            [a for c in chunks for a in back_pieces[c]],
            pre_gate,
            pre_linear,
            out_pair,
            (*gate_pair, *linear_pair),
            tile,
        )
        groups.append((x, b, gate_delta, linear_delta, hid))
        for i, c in enumerate(chunks):
            mine = rows[i * inner : (i + 1) * inner]
            home = [mine[0]] + [across(mine[k], k) for k in range(1, inner)]
            part = expand(metas[c], home, BF if c else F32)
            partial[c] = along(part, -c) if c else part
    theirs = weight_grads(groups, 1, (), tile)
    grads = weight_grads(groups, 0, [swap(a) for a in theirs], tile)

    total = partial[0]
    for c in range(1, PLANES):
        total = total + partial[c].astype(F32)
    latent_grad = join(total).astype(BF)
    side = latent_grad.shape[1] // 2
    token_grad = lax.dot_general(
        latent_grad[:, :side], down_pair[0], LAST, preferred_element_type=F32
    ) + lax.dot_general(latent_grad[:, side:], down_pair[1], LAST, preferred_element_type=F32)
    return (token_grad.astype(BF), grads[0][None], grads[1][None], grads[2][None])


def solution(mesh):
    in_specs = (
        P(("expert", "dp"), "half"),
        P(("expert", "dp"), "half"),
        P(("expert", "dp"), None),
        P(("expert", "dp"), None),
        P(("expert", "dp"), None),
        P("half", "dp"),
        P("dp", "half"),
        P("expert", "dp", "half"),
        P("expert", "dp", "half"),
        P("expert", "half", "dp"),
    )
    out_specs = (
        P(("expert", "dp"), "half"),
        P("expert", "dp", "half"),
        P("expert", "dp", "half"),
        P("expert", "half", "dp"),
    )
    return jax.shard_map(
        on_device, mesh=mesh, in_specs=in_specs, out_specs=out_specs, check_vma=False
    )
```

time: 304 us -> 270 us (0.89); the launches traced: 298 us -> 269 us
  Pallas kernels: 0 us -> 108 us
  waiting for transfers between devices: 139 us -> 67.7 us
  matrix products: 83.1 us -> 15.6 us
  starting transfers between devices: 30.5 us -> 71.4 us
  local copies, waits for them, and re-layouts: 20.2 us -> 1.39 us
  between operations: 14.4 us -> 1.32 us
  other arithmetic: 10.6 us -> 3.25 us
    all_to_all x3 -> x0, waiting for transfers between devices: 119 us -> none  [the longest x1 46.7 us: on_device(): lax.all_to_all(row_whole, 'expert', split_axis=0, concat_axis=0, tiled=True)]
    pallas_call x0 -> x18, Pallas kernels: none -> 108 us  [the longest x2 36.2 us: backward(): pl.pallas_call(functools.partial(backward_body, count, cap, padded), grid...]
    ppermute x0 -> x59, starting transfers between devices: none -> 71.4 us  [the longest x36 45.5 us: across(): return lax.ppermute(a, 'expert', [(i, i ^ k) for i in range(group_count)])]
    ppermute x0 -> x59, waiting for transfers between devices: none -> 67.7 us  [the longest x12 45.2 us: along(): lax.ppermute(a, 'expert', [(z * inner + p, (z + shift) % PLANES * inner +...]
    dot_general x11 -> x6, matrix products: 83.1 us -> 15.6 us  [the longest x4 9.48 us: dot(): lax.dot_general(a, weight, dims, preferred_element_type=F32)]
    all_to_all x3 -> x0, starting transfers between devices: 29.8 us -> none  [the longest x1 11.8 us: on_device(): lax.all_to_all(send_latent, 'expert', split_axis=0, concat_axis=0, tiled=...]
    gather x4 -> x0, local copies, waits for them, and re-layouts: 19.4 us -> none  [the longest x1 5.36 us: on_device(): gathered = returned.reshape(expert_count * capacity, width)[position]]
    all_gather x5 -> x0, waiting for transfers between devices: 17.1 us -> none  [the longest x1 17 us: on_device(): lax.all_gather(latent_up, 'dp', axis=0, tiled=True)]
  transfers between devices with their start and end apart: 11 -> 59, of which waited for: 4 -> 17; matrix products, arithmetic and copies ran while one was open for 31% -> 5% of each run, Pallas kernels for 0% -> 40%
where the time goes in v1:
time: 270 us; the launch traced here: 269 us
  Pallas kernels  108 us (40%)
  starting transfers between devices  71.4 us (26%)
  waiting for transfers between devices  67.7 us (25%)
  matrix products  15.6 us (6%)
  other arithmetic  3.25 us (1%)
    ppermute x36, starting transfers between devices, across(): return lax.ppermute(a, 'expert', [(i, i ^ k) for i in range(group_count)])  45.5 us
    ppermute x12, waiting for transfers between devices, along(): lax.ppermute(a, 'expert', [(z * inner + p, (z + shift) % PLANES * inner +...  45.2 us
    pallas_call x2, Pallas kernels, backward(): pl.pallas_call(functools.partial(backward_body, count, cap, padded), grid...  36.2 us
    pallas_call x2, Pallas kernels, weight_grads(): pl.pallas_call(functools.partial(weight_body, len(groups), bool(received)...  25.8 us
    ppermute x12, starting transfers between devices, along(): lax.ppermute(a, 'expert', [(z * inner + p, (z + shift) % PLANES * inner +...  24 us
    ppermute x36, waiting for transfers between devices, across(): return lax.ppermute(a, 'expert', [(i, i ^ k) for i in range(group_count)])  22.1 us
    pallas_call x2, Pallas kernels, forward(): pl.pallas_call(functools.partial(forward_body, count, cap, padded), grid=...  20.1 us
    pallas_call x8, Pallas kernels, select(): pl.pallas_call(functools.partial(select_body, picks, inner, cap, padded,...  16.8 us
  transfers between devices with their start and end apart: 59, of which 17 were waited for; matrix products, arithmetic and copies ran while one was open for 5% of the time, Pallas kernels for 40%

profile of v1, /device:TPU:0, one launch (start us, length us, event | category | flops | bytes accessed | tf_op | source)
XLA Modules:
  0.0 268.5 jit_solution(14625253085488712236)
XLA Ops:
  1.2 3.5 %convolution_convert_fusion.1 = bf16[128,512]{1,0:T(8,128)(2,1)S(1)} fusion(bf16[128,4096]{1,0:T(8,128)(2,1)} %param.10, bf16[4096,512]{1,0:T(8,128)(2,1)} %param.15), kind=kOutput, calls=%fused_computation.3 | convolution fusion | flops 536936448 | bytes 5373952 | tf_op jit(solution)/shard_map/dot_general | solution.py:324
  7.8 2.1 select_latent.4
  9.8 2.9 %collective-permute-start.12 = (bf16[72,1024]{1,0:T(8,128)(2,1)}, bf16[72,1024]{1,0:T(8,128)(2,1)S(1)}, u32[]{:S(2)}, u32[]{:S(2)}) collective-permute-start(bf16[72,1024]{1,0:T(8,128)(2,1)} %get-tuple-element.81), channel_id=1, source_target_pairs={{0,2},{2,0},{4,6},{6,4},{8,10},{10,8},{12,14},{14,12},{16,18},{18,... | collective-permute-start | bytes 442376 | tf_op jit(solution)/shard_map/ppermute | solution.py:313
  12.7 3.7 %convolution_convert_fusion.2 = bf16[128,512]{1,0:T(8,128)(2,1)S(1)} fusion(bf16[128,4096]{1,0:T(8,128)(2,1)S(1)} %collective-permute-done, bf16[512,4096]{1,0:T(8,128)(2,1)} %param.16), kind=kOutput, calls=%fused_computation.4 | convolution fusion | flops 536936448 | bytes 5373952 | tf_op jit(solution)/shard_map/dot_general | solution.py:324
  16.6 1.8 collective-permute-start.5
  18.3 2.6 collective-permute-start.29
  22.9 1.7 collective-permute-done.34.meta_ref
  24.6 1.6 collective-permute-start.13
  26.8 1.5 convolution_convert_fusion.3
  29.1 2.1 select_back.4
  31.2 3.0 %collective-permute-done.13.refs_2_ = bf16[72,1024]{1,0:T(8,128)(2,1)S(1)} collective-permute-done((bf16[72,1024]{1,0:T(8,128)(2,1)}, bf16[72,1024]{1,0:T(8,128)(2,1)S(1)}, u32[]{:S(2)}, u32[]{:S(2)}) %collective-permute-start.13) | collective-permute-done | bytes 147488 | tf_op jit(solution)/shard_map/ppermute | solution.py:313
  34.9 1.5 collective-permute-start.3
  36.4 3.4 %collective-permute-done.2.refs_1_ = bf16[72,1024]{1,0:T(8,128)(2,1)S(1)} collective-permute-done((bf16[72,1024]{1,0:T(8,128)(2,1)}, bf16[72,1024]{1,0:T(8,128)(2,1)S(1)}, u32[]{:S(2)}, u32[]{:S(2)}) %collective-permute-start.2) | collective-permute-done | bytes 147488 | tf_op jit(solution)/shard_map/ppermute | solution.py:313
  39.8 1.7 collective-permute-start.4
  41.6 4.4 %collective-permute-done.4.refs_3_ = bf16[72,1024]{1,0:T(8,128)(2,1)S(1)} collective-permute-done((bf16[72,1024]{1,0:T(8,128)(2,1)}, bf16[72,1024]{1,0:T(8,128)(2,1)S(1)}, u32[]{:S(2)}, u32[]{:S(2)}) %collective-permute-start.4) | collective-permute-done | bytes 147488 | tf_op jit(solution)/shard_map/ppermute | solution.py:313
  46.1 5.7 %collective-permute-done.15.block_ref = bf16[128,1024]{1,0:T(8,128)(2,1)S(1)} collective-permute-done((bf16[128,1024]{1,0:T(8,128)(2,1)S(1)}, bf16[128,1024]{1,0:T(8,128)(2,1)S(1)}, u32[]{:S(2)}, u32[]{:S(2)}) %collective-permute-start.15) | collective-permute-done | bytes 262176 | tf_op jit(solution)/shard_map/ppermute | solution.py:302
  51.8 5.6 %collective-permute-done.6.block_ref = bf16[128,1024]{1,0:T(8,128)(2,1)S(1)} collective-permute-done((bf16[128,1024]{1,0:T(8,128)(2,1)}, bf16[128,1024]{1,0:T(8,128)(2,1)S(1)}, u32[]{:S(2)}, u32[]{:S(2)}) %collective-permute-start.6) | collective-permute-done | bytes 262176 | tf_op jit(solution)/shard_map/ppermute | solution.py:302
  58.5 8.5 %collective-permute-done.39.block_ref = bf16[128,1024]{1,0:T(8,128)(2,1)S(1)} collective-permute-done((bf16[128,1024]{1,0:T(8,128)(2,1)S(1)}, bf16[128,1024]{1,0:T(8,128)(2,1)S(1)}, u32[]{:S(2)}, u32[]{:S(2)}) %collective-permute-start.39) | collective-permute-done | bytes 262176 | tf_op jit(solution)/shard_map/ppermute | solution.py:302
  67.7 2.5 collective-permute-done.43.block_ref
  70.2 10.4 %collective-permute-start.35 = (bf16[128,1024]{1,0:T(8,128)(2,1)}, bf16[128,1024]{1,0:T(8,128)(2,1)S(1)}, u32[]{:S(2)}, u32[]{:S(2)}) collective-permute-start(bf16[128,1024]{1,0:T(8,128)(2,1)} %pad_maximum_fusion.block_ref), channel_id=1, source_target_pairs={{0,24},{2,26},{4,28},{6,30},{8,0},{10,2},{12,4},{14,6},{16,8},{18,... | collective-permute-start | bytes 786440 | tf_op jit(solution)/shard_map/ppermute | solution.py:302
  80.6 2.1 select_latent.5
  82.6 2.9 %collective-permute-done.30.block_ref = bf16[128,1024]{1,0:T(8,128)(2,1)S(1)} collective-permute-done((bf16[128,1024]{1,0:T(8,128)(2,1)}, bf16[128,1024]{1,0:T(8,128)(2,1)S(1)}, u32[]{:S(2)}, u32[]{:S(2)}) %collective-permute-start.30) | collective-permute-done | bytes 262176 | tf_op jit(solution)/shard_map/ppermute | solution.py:302
  86.9 2.2 select_back.5
  89.6 1.6 collective-permute-start.18
  93.1 1.6 collective-permute-start.9
  94.8 2.1 select_latent.6
  96.9 2.1 select_back.6
  99.0 2.1 select_latent.7
  101.1 2.1 select_back.7
  103.2 1.4 collective-permute-start.40
  105.1 1.6 collective-permute-start.42
  106.8 1.4 collective-permute-start.44
  108.7 10.1 %forward_rows.2 = (bf16[640,1024]{1,0:T(8,128)(2,1)}, f32[640,1536]{1,0:T(8,128)}, f32[640,1536]{1,0:T(8,128)}) custom-call(bf16[72,1024]{1,0:T(8,128)(2,1)} %get-tuple-element.80.refs_0_, bf16[72,1024]{1,0:T(8,128)(2,1)} %copy-done.31, bf16[72,1024]{1,0:T(8,128)(2,1)} %copy-done.35, bf16[72,1024]{1,0:T(8,128)(2,1)} %copy-done.36, ...), custom_call_target="tpu_custom_call" | custom-call | flops 4026531840 | bytes 14155776 | tf_op jit(solution)/shard_map/forward_rows/pallas_call | solution.py:133
  119.0 1.7 collective-permute-start.46
  120.7 1.4 collective-permute-start.31
  122.7 1.7 collective-permute-start.33
  124.4 18.1 %backward_rows.2 = (bf16[640,1024]{1,0:T(8,128)(2,1)}, bf16[640,1536]{1,0:T(8,128)(2,1)}, bf16[640,1536]{1,0:T(8,128)(2,1)}, bf16[640,1536]{1,0:T(8,128)(2,1)}, ...) custom-call(bf16[72,1024]{1,0:T(8,128)(2,1)} %get-tuple-element.72.r, ...), custom_call_target="tpu_custom_call" | custom-call | flops 6039797760 | bytes 23199744 | tf_op jit(solution)/shard_map/backward_rows/pallas_call | solution.py:205
  142.6 1.4 collective-permute-start.36
  144.6 1.7 collective-permute-start.38
  146.3 1.4 collective-permute-start.25
  147.7 10.0 %forward_rows.3 = (bf16[640,1024]{1,0:T(8,128)(2,1)}, f32[640,1536]{1,0:T(8,128)}, f32[640,1536]{1,0:T(8,128)}) custom-call(bf16[72,1024]{1,0:T(8,128)(2,1)} %get-tuple-element.106.refs_0_, bf16[72,1024]{1,0:T(8,128)(2,1)} %copy-done.44, bf16[72,1024]{1,0:T(8,128)(2,1)} %copy-done.48, bf16[72,1024]{1,0:T(8,128)(2,1)} %copy-done.52, ...), custom_call_target="tpu_custom_call" | custom-call | flops 4026531840 | bytes 14155776 | tf_op jit(solution)/shard_map/forward_rows/pallas_call | solution.py:133
  158.3 1.7 collective-permute-start.27
  160.0 1.4 collective-permute-start.22
  162.0 18.1 %backward_rows.3 = (bf16[640,1024]{1,0:T(8,128)(2,1)}, bf16[640,1536]{1,0:T(8,128)(2,1)}, bf16[640,1536]{1,0:T(8,128)(2,1)}, bf16[640,1536]{1,0:T(8,128)(2,1)}, ...) custom-call(bf16[72,1024]{1,0:T(8,128)(2,1)} %get-tuple-element.98.r, ...), custom_call_target="tpu_custom_call" | custom-call | flops 6039797760 | bytes 23199744 | tf_op jit(solution)/shard_map/backward_rows/pallas_call | solution.py:205
  180.1 1.7 collective-permute-start.24
  181.8 1.4 collective-permute-start.47
  183.7 1.6 collective-permute-start.49
  185.4 12.3 %weight_grads.2 = (bf16[512,1536]{1,0:T(8,128)(2,1)}, bf16[512,1536]{1,0:T(8,128)(2,1)}, bf16[1536,512]{1,0:T(8,128)(2,1)}) custom-call(bf16[640,1024]{1,0:T(8,128)(2,1)} %get-tuple-element.124.refs_0_, bf16[640,1024]{1,0:T(8,128)(2,1)} %get-tuple-element.125.refs_1_, bf16[640,1536]{1,0:T(8,128)(2,1)} %get-tuple-element.126.refs_2_, ...), custom_call_target="tpu_custom_call" | custom-call | flops 6039797760 | bytes 16515072 | tf_op jit(solution)/shard_map/weight_grads/pallas_call | solution.py:260
  198.4 1.4 collective-permute-start.51
  199.9 4.8 %collective-permute-done.51.refs_1_ = bf16[72,1024]{1,0:T(8,128)(2,1)S(1)} collective-permute-done((bf16[72,1024]{1,0:T(8,128)(2,1)S(1)}, bf16[72,1024]{1,0:T(8,128)(2,1)S(1)}, u32[]{:S(2)}, u32[]{:S(2)}) %collective-permute-start.51) | collective-permute-done | bytes 147488 | tf_op jit(solution)/shard_map/ppermute | solution.py:313
  204.7 1.4 collective-permute-start.52
  206.1 3.9 %collective-permute-done.52.refs_2_ = bf16[72,1024]{1,0:T(8,128)(2,1)S(1)} collective-permute-done((bf16[72,1024]{1,0:T(8,128)(2,1)S(1)}, bf16[72,1024]{1,0:T(8,128)(2,1)S(1)}, u32[]{:S(2)}, u32[]{:S(2)}) %collective-permute-start.52) | collective-permute-done | bytes 147488 | tf_op jit(solution)/shard_map/ppermute | solution.py:313
  211.4 2.2 expand_rows.5
  213.6 2.5 collective-permute-done.53.refs_3_
  216.1 5.2 %collective-permute-start.28 = (bf16[128,1024]{1,0:T(8,128)(2,1)}, bf16[128,1024]{1,0:T(8,128)(2,1)S(1)}, u32[]{:S(2)}, u32[]{:S(2)}) collective-permute-start(bf16[128,1024]{1,0:T(8,128)(2,1)} %expand_rows.5), channel_id=1, source_target_pairs={{0,24},{2,26},{4,28},{6,30},{8,0},{10,2},{12,4},{14,6},{16,8},{18,... | collective-permute-start | bytes 786440 | tf_op jit(solution)/shard_map/ppermute | solution.py:302
  221.4 2.2 expand_rows.6
  223.6 4.0 %collective-permute-done.28 = bf16[128,1024]{1,0:T(8,128)(2,1)S(1)} collective-permute-done((bf16[128,1024]{1,0:T(8,128)(2,1)}, bf16[128,1024]{1,0:T(8,128)(2,1)S(1)}, u32[]{:S(2)}, u32[]{:S(2)}) %collective-permute-start.28) | collective-permute-done | bytes 262176 | tf_op jit(solution)/shard_map/ppermute | solution.py:302
  227.6 2.2 expand_rows.7
  229.8 8.0 %collective-permute-done.50 = bf16[128,1024]{1,0:T(8,128)(2,1)S(1)} collective-permute-done((bf16[128,1024]{1,0:T(8,128)(2,1)}, bf16[128,1024]{1,0:T(8,128)(2,1)S(1)}, u32[]{:S(2)}, u32[]{:S(2)}) %collective-permute-start.50) | collective-permute-done | bytes 262176 | tf_op jit(solution)/shard_map/ppermute | solution.py:302
  238.5 2.3 expand_rows.4
  240.9 5.7 %collective-permute-done.54 = bf16[128,1024]{1,0:T(8,128)(2,1)S(1)} collective-permute-done((bf16[128,1024]{1,0:T(8,128)(2,1)}, bf16[128,1024]{1,0:T(8,128)(2,1)S(1)}, u32[]{:S(2)}, u32[]{:S(2)}) %collective-permute-start.54) | collective-permute-done | bytes 262176 | tf_op jit(solution)/shard_map/ppermute | solution.py:302
  248.9 13.5 %weight_grads.3 = (bf16[512,1536]{1,0:T(8,128)(2,1)}, bf16[512,1536]{1,0:T(8,128)(2,1)}, bf16[1536,512]{1,0:T(8,128)(2,1)}) custom-call(bf16[640,1024]{1,0:T(8,128)(2,1)} %get-tuple-element.124.refs_0_, bf16[640,1024]{1,0:T(8,128)(2,1)} %get-tuple-element.125.refs_1_, bf16[640,1536]{1,0:T(8,128)(2,1)} %get-tuple-element.126.refs_2_, ...), custom_call_target="tpu_custom_call" | custom-call | flops 6039797760 | bytes 16515072 | tf_op jit(solution)/shard_map/weight_grads/pallas_call | solution.py:260
  262.4 3.7 %fusion.1 = f32[128,4096]{1,0:T(8,128)S(1)} fusion(bf16[4096,512]{1,0:T(8,128)(2,1)} %collective-permute-done.55, bf16[128,1024]{1,0:T(8,128)(2,1)S(1)} %add_convert_fusion), kind=kOutput, calls=%fused_computation.9 | convolution fusion | flops 536870912 | bytes 6422528 | tf_op jit(solution)/shard_map/dot_general | solution.py:378
  266.1 2.5 fusion
  (223 shorter events, 22.4 us)
Async XLA Ops:
  0.6 4.2 %collective-permute-start.10 = (bf16[128,4096]{1,0:T(8,128)(2,1)}, bf16[128,4096]{1,0:T(8,128)(2,1)S(1)}, u32[]{:S(2)}, u32[]{:S(2)}) collective-permute-start(bf16[128,4096]{1,0:T(8,128)(2,1)} %param.10), channel_id=1, source_target_pairs={{0,1},{1,0},{2,3},{3,2},{4,5},{5,4},{6,7},{7,6},{8,9},{9,8},{10,11... | collective-permute-start | bytes 3145736 | tf_op jit(solution)/shard_map/ppermute | solution.py:299
  1.2 11.6 %collective-permute-start = (bf16[128,4096]{1,0:T(8,128)(2,1)}, bf16[128,4096]{1,0:T(8,128)(2,1)S(1)}, u32[]{:S(2)}, u32[]{:S(2)}) collective-permute-start(bf16[128,4096]{1,0:T(8,128)(2,1)} %param.11), channel_id=1, source_target_pairs={{0,1},{1,0},{2,3},{3,2},{4,5},{5,4},{6,7},{7,6},{8,9},{9,8},{10,11... | collective-permute-start | bytes 3145736 | tf_op jit(solution)/shard_map/ppermute | solution.py:299
  5.6 1.5 collective-permute-start.11
  9.8 16.3 %collective-permute-start.12 = (bf16[72,1024]{1,0:T(8,128)(2,1)}, bf16[72,1024]{1,0:T(8,128)(2,1)S(1)}, u32[]{:S(2)}, u32[]{:S(2)}) collective-permute-start(bf16[72,1024]{1,0:T(8,128)(2,1)} %get-tuple-element.81), channel_id=1, source_target_pairs={{0,2},{2,0},{4,6},{6,4},{8,10},{10,8},{12,14},{14,12},{16,18},{18,... | collective-permute-start | bytes 442376 | tf_op jit(solution)/shard_map/ppermute | solution.py:313
  16.5 8.1 %collective-permute-start.1 = (bf16[128,512]{1,0:T(8,128)(2,1)S(1)}, bf16[128,512]{1,0:T(8,128)(2,1)S(1)}, u32[]{:S(2)}, u32[]{:S(2)}) collective-permute-start(bf16[128,512]{1,0:T(8,128)(2,1)S(1)} %convolution_convert_fusion.2), channel_id=1, source_target_pairs={{0,1},{1,0},{2,3},{3,2},{4,5},{5,4},{6,7},{7,6},{8,9},{9,8},{10,11... | collective-permute-start | bytes 393224 | tf_op jit(solution)/shard_map/ppermute | solution.py:299
  16.6 5.7 %collective-permute-start.5 = (f32[16,128]{1,0:T(8,128)S(1)}, f32[16,128]{1,0:T(8,128)S(1)}, u32[]{:S(2)}, u32[]{:S(2)}) collective-permute-start(f32[16,128]{1,0:T(8,128)S(1)} %copy-done.16), channel_id=1, source_target_pairs={{0,8},{2,10},{4,12},{6,14},{8,16},{10,18},{12,20},{14,22},{16,24},... | collective-permute-start | bytes 24584 | tf_op jit(solution)/shard_map/ppermute | solution.py:302
  18.3 4.5 %collective-permute-start.29 = (f32[16,128]{1,0:T(8,128)S(1)}, f32[16,128]{1,0:T(8,128)S(1)}, u32[]{:S(2)}, u32[]{:S(2)}) collective-permute-start(f32[16,128]{1,0:T(8,128)S(1)} %copy-done.16), channel_id=1, source_target_pairs={{0,16},{2,18},{4,20},{6,22},{8,24},{10,26},{12,28},{14,30},{16,0},... | collective-permute-start | bytes 24584 | tf_op jit(solution)/shard_map/ppermute | solution.py:302
  20.9 3.7 %collective-permute-start.34 = (f32[16,128]{1,0:T(8,128)S(1)}, f32[16,128]{1,0:T(8,128)S(1)}, u32[]{:S(2)}, u32[]{:S(2)}) collective-permute-start(f32[16,128]{1,0:T(8,128)S(1)} %copy-done.16), channel_id=1, source_target_pairs={{0,24},{2,26},{4,28},{6,30},{8,0},{10,2},{12,4},{14,6},{16,8},{18,... | collective-permute-start | bytes 24584 | tf_op jit(solution)/shard_map/ppermute | solution.py:302
  22.3 67.4 %collective-permute-start.19 = (bf16[512,1536]{1,0:T(8,128)(2,1)S(1)}, bf16[512,1536]{1,0:T(8,128)(2,1)}, u32[]{:S(2)}, u32[]{:S(2)}) collective-permute-start(bf16[512,1536]{1,0:T(8,128)(2,1)S(1)} %bitcast.22), channel_id=1, source_target_pairs={{0,1},{1,0},{2,3},{3,2},{4,5},{5,4},{6,7},{7,6},{8,9},{9,8},{10,11... | collective-permute-start | bytes 4718600 | tf_op jit(solution)/shard_map/ppermute | solution.py:299
  22.9 68.4 %collective-permute-start.20 = (bf16[512,1536]{1,0:T(8,128)(2,1)}, bf16[512,1536]{1,0:T(8,128)(2,1)}, u32[]{:S(2)}, u32[]{:S(2)}) collective-permute-start(bf16[512,1536]{1,0:T(8,128)(2,1)} %bitcast.23), channel_id=1, source_target_pairs={{0,1},{1,0},{2,3},{3,2},{4,5},{5,4},{6,7},{7,6},{8,9},{9,8},{10,11... | collective-permute-start | bytes 4718600 | tf_op jit(solution)/shard_map/ppermute | solution.py:299
  24.6 68.1 %collective-permute-start.21 = (bf16[1536,512]{1,0:T(8,128)(2,1)}, bf16[1536,512]{1,0:T(8,128)(2,1)}, u32[]{:S(2)}, u32[]{:S(2)}) collective-permute-start(bf16[1536,512]{1,0:T(8,128)(2,1)} %bitcast.28), channel_id=1, source_target_pairs={{0,1},{1,0},{2,3},{3,2},{4,5},{5,4},{6,7},{7,6},{8,9},{9,8},{10,11... | collective-permute-start | bytes 4718600 | tf_op jit(solution)/shard_map/ppermute | solution.py:299
  24.6 9.6 %collective-permute-start.13 = (bf16[72,1024]{1,0:T(8,128)(2,1)}, bf16[72,1024]{1,0:T(8,128)(2,1)S(1)}, u32[]{:S(2)}, u32[]{:S(2)}) collective-permute-start(bf16[72,1024]{1,0:T(8,128)(2,1)} %get-tuple-element.82), channel_id=1, source_target_pairs={{0,4},{2,6},{4,0},{6,2},{8,12},{10,14},{12,8},{14,10},{16,20},{18,... | collective-permute-start | bytes 442376 | tf_op jit(solution)/shard_map/ppermute | solution.py:313
  26.2 8.7 %collective-permute-start.14 = (bf16[72,1024]{1,0:T(8,128)(2,1)}, bf16[72,1024]{1,0:T(8,128)(2,1)S(1)}, u32[]{:S(2)}, u32[]{:S(2)}) collective-permute-start(bf16[72,1024]{1,0:T(8,128)(2,1)} %get-tuple-element.83), channel_id=1, source_target_pairs={{0,6},{2,4},{4,2},{6,0},{8,14},{10,12},{12,10},{14,8},{16,22},{18,... | collective-permute-start | bytes 442376 | tf_op jit(solution)/shard_map/ppermute | solution.py:313
  34.2 74.4 %copy-start.35 = (bf16[72,1024]{1,0:T(8,128)(2,1)}, bf16[72,1024]{1,0:T(8,128)(2,1)S(1)}, u32[]{:S(2)}) copy-start(bf16[72,1024]{1,0:T(8,128)(2,1)S(1)} %collective-permute-done.13.refs_2_) | copy-start | bytes 442372
  34.2 5.6 %collective-permute-start.2 = (bf16[72,1024]{1,0:T(8,128)(2,1)}, bf16[72,1024]{1,0:T(8,128)(2,1)S(1)}, u32[]{:S(2)}, u32[]{:S(2)}) collective-permute-start(bf16[72,1024]{1,0:T(8,128)(2,1)} %get-tuple-element.73), channel_id=1, source_target_pairs={{0,2},{2,0},{4,6},{6,4},{8,10},{10,8},{12,14},{14,12},{16,18},{18,... | collective-permute-start | bytes 442376 | tf_op jit(solution)/shard_map/ppermute | solution.py:313
  34.9 73.7 %copy-start.36 = (bf16[72,1024]{1,0:T(8,128)(2,1)}, bf16[72,1024]{1,0:T(8,128)(2,1)S(1)}, u32[]{:S(2)}) copy-start(bf16[72,1024]{1,0:T(8,128)(2,1)S(1)} %collective-permute-done.14.refs_3_) | copy-start | bytes 442372
  34.9 6.6 %collective-permute-start.3 = (bf16[72,1024]{1,0:T(8,128)(2,1)}, bf16[72,1024]{1,0:T(8,128)(2,1)S(1)}, u32[]{:S(2)}, u32[]{:S(2)}) collective-permute-start(bf16[72,1024]{1,0:T(8,128)(2,1)} %get-tuple-element.74), channel_id=1, source_target_pairs={{0,4},{2,6},{4,0},{6,2},{8,12},{10,14},{12,8},{14,10},{16,20},{18,... | collective-permute-start | bytes 442376 | tf_op jit(solution)/shard_map/ppermute | solution.py:313
  39.8 79.0 %copy-start.32 = (bf16[72,1024]{1,0:T(8,128)(2,1)}, bf16[72,1024]{1,0:T(8,128)(2,1)S(1)}, u32[]{:S(2)}) copy-start(bf16[72,1024]{1,0:T(8,128)(2,1)S(1)} %collective-permute-done.2.refs_1_) | copy-start | bytes 442372
  39.8 6.3 %collective-permute-start.4 = (bf16[72,1024]{1,0:T(8,128)(2,1)}, bf16[72,1024]{1,0:T(8,128)(2,1)S(1)}, u32[]{:S(2)}, u32[]{:S(2)}) collective-permute-start(bf16[72,1024]{1,0:T(8,128)(2,1)} %get-tuple-element.75), channel_id=1, source_target_pairs={{0,6},{2,4},{4,2},{6,0},{8,14},{10,12},{12,10},{14,8},{16,22},{18,... | collective-permute-start | bytes 442376 | tf_op jit(solution)/shard_map/ppermute | solution.py:313
  41.5 77.4 %copy-start.33 = (bf16[72,1024]{1,0:T(8,128)(2,1)}, bf16[72,1024]{1,0:T(8,128)(2,1)S(1)}, u32[]{:S(2)}) copy-start(bf16[72,1024]{1,0:T(8,128)(2,1)S(1)} %collective-permute-done.3.refs_2_) | copy-start | bytes 442372
  41.5 10.3 %collective-permute-start.15 = (bf16[128,1024]{1,0:T(8,128)(2,1)S(1)}, bf16[128,1024]{1,0:T(8,128)(2,1)S(1)}, u32[]{:S(2)}, u32[]{:S(2)}) collective-permute-start(bf16[128,1024]{1,0:T(8,128)(2,1)S(1)} %copy-done.3), channel_id=1, source_target_pairs={{0,8},{2,10},{4,12},{6,14},{8,16},{10,18},{12,20},{14,22},{16,24},... | collective-permute-start | bytes 786440 | tf_op jit(solution)/shard_map/ppermute | solution.py:302
  46.1 72.8 %copy-start.34 = (bf16[72,1024]{1,0:T(8,128)(2,1)}, bf16[72,1024]{1,0:T(8,128)(2,1)S(1)}, u32[]{:S(2)}) copy-start(bf16[72,1024]{1,0:T(8,128)(2,1)S(1)} %collective-permute-done.4.refs_3_) | copy-start | bytes 442372
  46.1 11.3 %collective-permute-start.6 = (bf16[128,1024]{1,0:T(8,128)(2,1)}, bf16[128,1024]{1,0:T(8,128)(2,1)S(1)}, u32[]{:S(2)}, u32[]{:S(2)}) collective-permute-start(bf16[128,1024]{1,0:T(8,128)(2,1)} %pad_maximum_fusion.block_ref), channel_id=1, source_target_pairs={{0,8},{2,10},{4,12},{6,14},{8,16},{10,18},{12,20},{14,22},{16,24},... | collective-permute-start | bytes 786440 | tf_op jit(solution)/shard_map/ppermute | solution.py:302
  51.8 15.2 %collective-permute-start.39 = (bf16[128,1024]{1,0:T(8,128)(2,1)S(1)}, bf16[128,1024]{1,0:T(8,128)(2,1)S(1)}, u32[]{:S(2)}, u32[]{:S(2)}) collective-permute-start(bf16[128,1024]{1,0:T(8,128)(2,1)S(1)} %copy-done.3), channel_id=1, source_target_pairs={{0,16},{2,18},{4,20},{6,22},{8,24},{10,26},{12,28},{14,30},{16,0},... | collective-permute-start | bytes 786440 | tf_op jit(solution)/shard_map/ppermute | solution.py:302
  57.4 12.7 %collective-permute-start.43 = (bf16[128,1024]{1,0:T(8,128)(2,1)S(1)}, bf16[128,1024]{1,0:T(8,128)(2,1)S(1)}, u32[]{:S(2)}, u32[]{:S(2)}) collective-permute-start(bf16[128,1024]{1,0:T(8,128)(2,1)S(1)} %copy-done.3), channel_id=1, source_target_pairs={{0,24},{2,26},{4,28},{6,30},{8,0},{10,2},{12,4},{14,6},{16,8},{18,... | collective-permute-start | bytes 786440 | tf_op jit(solution)/shard_map/ppermute | solution.py:302
  67.0 18.6 %collective-permute-start.30 = (bf16[128,1024]{1,0:T(8,128)(2,1)}, bf16[128,1024]{1,0:T(8,128)(2,1)S(1)}, u32[]{:S(2)}, u32[]{:S(2)}) collective-permute-start(bf16[128,1024]{1,0:T(8,128)(2,1)} %pad_maximum_fusion.block_ref), channel_id=1, source_target_pairs={{0,16},{2,18},{4,20},{6,22},{8,24},{10,26},{12,28},{14,30},{16,0},... | collective-permute-start | bytes 786440 | tf_op jit(solution)/shard_map/ppermute | solution.py:302
  70.2 18.9 %collective-permute-start.35 = (bf16[128,1024]{1,0:T(8,128)(2,1)}, bf16[128,1024]{1,0:T(8,128)(2,1)S(1)}, u32[]{:S(2)}, u32[]{:S(2)}) collective-permute-start(bf16[128,1024]{1,0:T(8,128)(2,1)} %pad_maximum_fusion.block_ref), channel_id=1, source_target_pairs={{0,24},{2,26},{4,28},{6,30},{8,0},{10,2},{12,4},{14,6},{16,8},{18,... | collective-permute-start | bytes 786440 | tf_op jit(solution)/shard_map/ppermute | solution.py:302
  85.6 7.6 %collective-permute-start.16 = (bf16[72,1024]{1,0:T(8,128)(2,1)}, bf16[72,1024]{1,0:T(8,128)(2,1)S(1)}, u32[]{:S(2)}, u32[]{:S(2)}) collective-permute-start(bf16[72,1024]{1,0:T(8,128)(2,1)} %get-tuple-element.85), channel_id=1, source_target_pairs={{0,2},{2,0},{4,6},{6,4},{8,10},{10,8},{12,14},{14,12},{16,18},{18,... | collective-permute-start | bytes 442376 | tf_op jit(solution)/shard_map/ppermute | solution.py:313
  89.1 14.1 %collective-permute-start.17 = (bf16[72,1024]{1,0:T(8,128)(2,1)}, bf16[72,1024]{1,0:T(8,128)(2,1)S(1)}, u32[]{:S(2)}, u32[]{:S(2)}) collective-permute-start(bf16[72,1024]{1,0:T(8,128)(2,1)} %get-tuple-element.86), channel_id=1, source_target_pairs={{0,4},{2,6},{4,0},{6,2},{8,12},{10,14},{12,8},{14,10},{16,20},{18,... | collective-permute-start | bytes 442376 | tf_op jit(solution)/shard_map/ppermute | solution.py:313
  89.6 15.0 %collective-permute-start.18 = (bf16[72,1024]{1,0:T(8,128)(2,1)}, bf16[72,1024]{1,0:T(8,128)(2,1)S(1)}, u32[]{:S(2)}, u32[]{:S(2)}) collective-permute-start(bf16[72,1024]{1,0:T(8,128)(2,1)} %get-tuple-element.87), channel_id=1, source_target_pairs={{0,6},{2,4},{4,2},{6,0},{8,14},{10,12},{12,10},{14,8},{16,22},{18,... | collective-permute-start | bytes 442376 | tf_op jit(solution)/shard_map/ppermute | solution.py:313
  91.3 13.9 %collective-permute-start.7 = (bf16[72,1024]{1,0:T(8,128)(2,1)}, bf16[72,1024]{1,0:T(8,128)(2,1)S(1)}, u32[]{:S(2)}, u32[]{:S(2)}) collective-permute-start(bf16[72,1024]{1,0:T(8,128)(2,1)} %get-tuple-element.77), channel_id=1, source_target_pairs={{0,2},{2,0},{4,6},{6,4},{8,10},{10,8},{12,14},{14,12},{16,18},{18,... | collective-permute-start | bytes 442376 | tf_op jit(solution)/shard_map/ppermute | solution.py:313
  92.6 14.1 %collective-permute-start.8 = (bf16[72,1024]{1,0:T(8,128)(2,1)}, bf16[72,1024]{1,0:T(8,128)(2,1)S(1)}, u32[]{:S(2)}, u32[]{:S(2)}) collective-permute-start(bf16[72,1024]{1,0:T(8,128)(2,1)} %get-tuple-element.78), channel_id=1, source_target_pairs={{0,4},{2,6},{4,0},{6,2},{8,12},{10,14},{12,8},{14,10},{16,20},{18,... | collective-permute-start | bytes 442376 | tf_op jit(solution)/shard_map/ppermute | solution.py:313
  93.1 15.0 %collective-permute-start.9 = (bf16[72,1024]{1,0:T(8,128)(2,1)}, bf16[72,1024]{1,0:T(8,128)(2,1)S(1)}, u32[]{:S(2)}, u32[]{:S(2)}) collective-permute-start(bf16[72,1024]{1,0:T(8,128)(2,1)} %get-tuple-element.79), channel_id=1, source_target_pairs={{0,6},{2,4},{4,2},{6,0},{8,14},{10,12},{12,10},{14,8},{16,22},{18,... | collective-permute-start | bytes 442376 | tf_op jit(solution)/shard_map/ppermute | solution.py:313
  103.2 15.7 %collective-permute-start.40 = (bf16[72,1024]{1,0:T(8,128)(2,1)}, bf16[72,1024]{1,0:T(8,128)(2,1)S(1)}, u32[]{:S(2)}, u32[]{:S(2)}) collective-permute-start(bf16[72,1024]{1,0:T(8,128)(2,1)} %get-tuple-element.107), channel_id=1, source_target_pairs={{0,2},{2,0},{4,6},{6,4},{8,10},{10,8},{12,14},{14,12},{16,18},{18,... | collective-permute-start | bytes 442376 | tf_op jit(solution)/shard_map/ppermute | solution.py:313
  104.6 14.3 %collective-permute-start.41 = (bf16[72,1024]{1,0:T(8,128)(2,1)}, bf16[72,1024]{1,0:T(8,128)(2,1)S(1)}, u32[]{:S(2)}, u32[]{:S(2)}) collective-permute-start(bf16[72,1024]{1,0:T(8,128)(2,1)} %get-tuple-element.108), channel_id=1, source_target_pairs={{0,4},{2,6},{4,0},{6,2},{8,12},{10,14},{12,8},{14,10},{16,20},{18,... | collective-permute-start | bytes 442376 | tf_op jit(solution)/shard_map/ppermute | solution.py:313
  105.1 15.6 %collective-permute-start.42 = (bf16[72,1024]{1,0:T(8,128)(2,1)}, bf16[72,1024]{1,0:T(8,128)(2,1)S(1)}, u32[]{:S(2)}, u32[]{:S(2)}) collective-permute-start(bf16[72,1024]{1,0:T(8,128)(2,1)} %get-tuple-element.109), channel_id=1, source_target_pairs={{0,6},{2,4},{4,2},{6,0},{8,14},{10,12},{12,10},{14,8},{16,22},{18,... | collective-permute-start | bytes 442376 | tf_op jit(solution)/shard_map/ppermute | solution.py:313
  106.8 15.4 %collective-permute-start.44 = (bf16[72,1024]{1,0:T(8,128)(2,1)}, bf16[72,1024]{1,0:T(8,128)(2,1)S(1)}, u32[]{:S(2)}, u32[]{:S(2)}) collective-permute-start(bf16[72,1024]{1,0:T(8,128)(2,1)} %get-tuple-element.111), channel_id=1, source_target_pairs={{0,2},{2,0},{4,6},{6,4},{8,10},{10,8},{12,14},{14,12},{16,18},{18,... | collective-permute-start | bytes 442376 | tf_op jit(solution)/shard_map/ppermute | solution.py:313
  108.2 14.6 %collective-permute-start.45 = (bf16[72,1024]{1,0:T(8,128)(2,1)}, bf16[72,1024]{1,0:T(8,128)(2,1)S(1)}, u32[]{:S(2)}, u32[]{:S(2)}) collective-permute-start(bf16[72,1024]{1,0:T(8,128)(2,1)} %get-tuple-element.112), channel_id=1, source_target_pairs={{0,4},{2,6},{4,0},{6,2},{8,12},{10,14},{12,8},{14,10},{16,20},{18,... | collective-permute-start | bytes 442376 | tf_op jit(solution)/shard_map/ppermute | solution.py:313
  118.9 143.5 %collective-permute-start.55 = (bf16[4096,512]{1,0:T(8,128)(2,1)S(1)}, bf16[4096,512]{1,0:T(8,128)(2,1)}, u32[]{:S(2)}, u32[]{:S(2)}) collective-permute-start(bf16[4096,512]{1,0:T(8,128)(2,1)S(1)} %copy-done), channel_id=1, source_target_pairs={{0,1},{1,0},{2,3},{3,2},{4,5},{5,4},{6,7},{7,6},{8,9},{9,8},{10,11... | collective-permute-start | bytes 12582920 | tf_op jit(solution)/shard_map/ppermute | solution.py:299
  119.0 23.5 %collective-permute-start.46 = (bf16[72,1024]{1,0:T(8,128)(2,1)S(1)}, bf16[72,1024]{1,0:T(8,128)(2,1)S(1)}, u32[]{:S(2)}, u32[]{:S(2)}) collective-permute-start(bf16[72,1024]{1,0:T(8,128)(2,1)S(1)} %copy-done.56), channel_id=1, source_target_pairs={{0,6},{2,4},{4,2},{6,0},{8,14},{10,12},{12,10},{14,8},{16,22},{18,... | collective-permute-start | bytes 442376 | tf_op jit(solution)/shard_map/ppermute | solution.py:313
  120.7 23.3 %collective-permute-start.31 = (bf16[72,1024]{1,0:T(8,128)(2,1)S(1)}, bf16[72,1024]{1,0:T(8,128)(2,1)S(1)}, u32[]{:S(2)}, u32[]{:S(2)}) collective-permute-start(bf16[72,1024]{1,0:T(8,128)(2,1)S(1)} %copy-done.47), channel_id=1, source_target_pairs={{0,2},{2,0},{4,6},{6,4},{8,10},{10,8},{12,14},{14,12},{16,18},{18,... | collective-permute-start | bytes 442376 | tf_op jit(solution)/shard_map/ppermute | solution.py:313
  122.2 22.4 %collective-permute-start.32 = (bf16[72,1024]{1,0:T(8,128)(2,1)S(1)}, bf16[72,1024]{1,0:T(8,128)(2,1)S(1)}, u32[]{:S(2)}, u32[]{:S(2)}) collective-permute-start(bf16[72,1024]{1,0:T(8,128)(2,1)S(1)} %copy-done.43), channel_id=1, source_target_pairs={{0,4},{2,6},{4,0},{6,2},{8,12},{10,14},{12,8},{14,10},{16,20},{18,... | collective-permute-start | bytes 442376 | tf_op jit(solution)/shard_map/ppermute | solution.py:313
  122.7 23.6 %collective-permute-start.33 = (bf16[72,1024]{1,0:T(8,128)(2,1)S(1)}, bf16[72,1024]{1,0:T(8,128)(2,1)S(1)}, u32[]{:S(2)}, u32[]{:S(2)}) collective-permute-start(bf16[72,1024]{1,0:T(8,128)(2,1)S(1)} %copy-done.41), channel_id=1, source_target_pairs={{0,6},{2,4},{4,2},{6,0},{8,14},{10,12},{12,10},{14,8},{16,22},{18,... | collective-permute-start | bytes 442376 | tf_op jit(solution)/shard_map/ppermute | solution.py:313
  142.6 15.1 %collective-permute-start.36 = (bf16[72,1024]{1,0:T(8,128)(2,1)S(1)}, bf16[72,1024]{1,0:T(8,128)(2,1)S(1)}, u32[]{:S(2)}, u32[]{:S(2)}) collective-permute-start(bf16[72,1024]{1,0:T(8,128)(2,1)S(1)} %copy-done.39), channel_id=1, source_target_pairs={{0,2},{2,0},{4,6},{6,4},{8,10},{10,8},{12,14},{14,12},{16,18},{18,... | collective-permute-start | bytes 442376 | tf_op jit(solution)/shard_map/ppermute | solution.py:313
  144.0 14.2 %collective-permute-start.37 = (bf16[72,1024]{1,0:T(8,128)(2,1)S(1)}, bf16[72,1024]{1,0:T(8,128)(2,1)S(1)}, u32[]{:S(2)}, u32[]{:S(2)}) collective-permute-start(bf16[72,1024]{1,0:T(8,128)(2,1)S(1)} %copy-done.38), channel_id=1, source_target_pairs={{0,4},{2,6},{4,0},{6,2},{8,12},{10,14},{12,8},{14,10},{16,20},{18,... | collective-permute-start | bytes 442376 | tf_op jit(solution)/shard_map/ppermute | solution.py:313
  144.6 15.4 %collective-permute-start.38 = (bf16[72,1024]{1,0:T(8,128)(2,1)S(1)}, bf16[72,1024]{1,0:T(8,128)(2,1)S(1)}, u32[]{:S(2)}, u32[]{:S(2)}) collective-permute-start(bf16[72,1024]{1,0:T(8,128)(2,1)S(1)} %copy-done.37), channel_id=1, source_target_pairs={{0,6},{2,4},{4,2},{6,0},{8,14},{10,12},{12,10},{14,8},{16,22},{18,... | collective-permute-start | bytes 442376 | tf_op jit(solution)/shard_map/ppermute | solution.py:313
  146.3 15.1 %collective-permute-start.25 = (bf16[72,1024]{1,0:T(8,128)(2,1)}, bf16[72,1024]{1,0:T(8,128)(2,1)S(1)}, u32[]{:S(2)}, u32[]{:S(2)}) collective-permute-start(bf16[72,1024]{1,0:T(8,128)(2,1)} %get-tuple-element.95), channel_id=1, source_target_pairs={{0,2},{2,0},{4,6},{6,4},{8,10},{10,8},{12,14},{14,12},{16,18},{18,... | collective-permute-start | bytes 442376 | tf_op jit(solution)/shard_map/ppermute | solution.py:313
  157.7 22.4 %collective-permute-start.26 = (bf16[72,1024]{1,0:T(8,128)(2,1)S(1)}, bf16[72,1024]{1,0:T(8,128)(2,1)S(1)}, u32[]{:S(2)}, u32[]{:S(2)}) collective-permute-start(bf16[72,1024]{1,0:T(8,128)(2,1)S(1)} %copy-done.57), channel_id=1, source_target_pairs={{0,4},{2,6},{4,0},{6,2},{8,12},{10,14},{12,8},{14,10},{16,20},{18,... | collective-permute-start | bytes 442376 | tf_op jit(solution)/shard_map/ppermute | solution.py:313
  158.3 23.6 %collective-permute-start.27 = (bf16[72,1024]{1,0:T(8,128)(2,1)S(1)}, bf16[72,1024]{1,0:T(8,128)(2,1)S(1)}, u32[]{:S(2)}, u32[]{:S(2)}) collective-permute-start(bf16[72,1024]{1,0:T(8,128)(2,1)S(1)} %copy-done.53), channel_id=1, source_target_pairs={{0,6},{2,4},{4,2},{6,0},{8,14},{10,12},{12,10},{14,8},{16,22},{18,... | collective-permute-start | bytes 442376 | tf_op jit(solution)/shard_map/ppermute | solution.py:313
  160.0 23.2 %collective-permute-start.22 = (bf16[72,1024]{1,0:T(8,128)(2,1)S(1)}, bf16[72,1024]{1,0:T(8,128)(2,1)S(1)}, u32[]{:S(2)}, u32[]{:S(2)}) collective-permute-start(bf16[72,1024]{1,0:T(8,128)(2,1)S(1)} %copy-done.49), channel_id=1, source_target_pairs={{0,2},{2,0},{4,6},{6,4},{8,10},{10,8},{12,14},{14,12},{16,18},{18,... | collective-permute-start | bytes 442376 | tf_op jit(solution)/shard_map/ppermute | solution.py:313
  161.4 22.3 %collective-permute-start.23 = (bf16[72,1024]{1,0:T(8,128)(2,1)S(1)}, bf16[72,1024]{1,0:T(8,128)(2,1)S(1)}, u32[]{:S(2)}, u32[]{:S(2)}) collective-permute-start(bf16[72,1024]{1,0:T(8,128)(2,1)S(1)} %copy-done.45), channel_id=1, source_target_pairs={{0,4},{2,6},{4,0},{6,2},{8,12},{10,14},{12,8},{14,10},{16,20},{18,... | collective-permute-start | bytes 442376 | tf_op jit(solution)/shard_map/ppermute | solution.py:313
  180.1 17.6 %collective-permute-start.24 = (bf16[72,1024]{1,0:T(8,128)(2,1)S(1)}, bf16[72,1024]{1,0:T(8,128)(2,1)S(1)}, u32[]{:S(2)}, u32[]{:S(2)}) collective-permute-start(bf16[72,1024]{1,0:T(8,128)(2,1)S(1)} %copy-done.40), channel_id=1, source_target_pairs={{0,6},{2,4},{4,2},{6,0},{8,14},{10,12},{12,10},{14,8},{16,22},{18,... | collective-permute-start | bytes 442376 | tf_op jit(solution)/shard_map/ppermute | solution.py:313
  181.8 16.0 %collective-permute-start.47 = (bf16[72,1024]{1,0:T(8,128)(2,1)}, bf16[72,1024]{1,0:T(8,128)(2,1)S(1)}, u32[]{:S(2)}, u32[]{:S(2)}) collective-permute-start(bf16[72,1024]{1,0:T(8,128)(2,1)} %get-tuple-element.117), channel_id=1, source_target_pairs={{0,2},{2,0},{4,6},{6,4},{8,10},{10,8},{12,14},{14,12},{16,18},{18,... | collective-permute-start | bytes 442376 | tf_op jit(solution)/shard_map/ppermute | solution.py:313
  183.2 15.1 %collective-permute-start.48 = (bf16[72,1024]{1,0:T(8,128)(2,1)}, bf16[72,1024]{1,0:T(8,128)(2,1)S(1)}, u32[]{:S(2)}, u32[]{:S(2)}) collective-permute-start(bf16[72,1024]{1,0:T(8,128)(2,1)} %get-tuple-element.118), channel_id=1, source_target_pairs={{0,4},{2,6},{4,0},{6,2},{8,12},{10,14},{12,8},{14,10},{16,20},{18,... | collective-permute-start | bytes 442376 | tf_op jit(solution)/shard_map/ppermute | solution.py:313
  183.7 14.7 %collective-permute-start.49 = (bf16[72,1024]{1,0:T(8,128)(2,1)}, bf16[72,1024]{1,0:T(8,128)(2,1)S(1)}, u32[]{:S(2)}, u32[]{:S(2)}) collective-permute-start(bf16[72,1024]{1,0:T(8,128)(2,1)} %get-tuple-element.119), channel_id=1, source_target_pairs={{0,6},{2,4},{4,2},{6,0},{8,14},{10,12},{12,10},{14,8},{16,22},{18,... | collective-permute-start | bytes 442376 | tf_op jit(solution)/shard_map/ppermute | solution.py:313
  197.7 50.0 %collective-permute-start.56 = (bf16[512,1536]{1,0:T(8,128)(2,1)}, bf16[512,1536]{1,0:T(8,128)(2,1)S(1)}, u32[]{:S(2)}, u32[]{:S(2)}) collective-permute-start(bf16[512,1536]{1,0:T(8,128)(2,1)} %get-tuple-element.134), channel_id=1, source_target_pairs={{0,1},{1,0},{2,3},{3,2},{4,5},{5,4},{6,7},{7,6},{8,9},{9,8},{10,11... | collective-permute-start | bytes 4718600 | tf_op jit(solution)/shard_map/ppermute | solution.py:299
  197.8 50.0 %collective-permute-start.57 = (bf16[512,1536]{1,0:T(8,128)(2,1)}, bf16[512,1536]{1,0:T(8,128)(2,1)}, u32[]{:S(2)}, u32[]{:S(2)}) collective-permute-start(bf16[512,1536]{1,0:T(8,128)(2,1)} %get-tuple-element.135), channel_id=1, source_target_pairs={{0,1},{1,0},{2,3},{3,2},{4,5},{5,4},{6,7},{7,6},{8,9},{9,8},{10,11... | collective-permute-start | bytes 4718600 | tf_op jit(solution)/shard_map/ppermute | solution.py:299
  198.3 49.5 %collective-permute-start.58 = (bf16[1536,512]{1,0:T(8,128)(2,1)}, bf16[1536,512]{1,0:T(8,128)(2,1)}, u32[]{:S(2)}, u32[]{:S(2)}) collective-permute-start(bf16[1536,512]{1,0:T(8,128)(2,1)} %get-tuple-element.136), channel_id=1, source_target_pairs={{0,1},{1,0},{2,3},{3,2},{4,5},{5,4},{6,7},{7,6},{8,9},{9,8},{10,11... | collective-permute-start | bytes 4718600 | tf_op jit(solution)/shard_map/ppermute | solution.py:299
  198.4 6.2 %collective-permute-start.51 = (bf16[72,1024]{1,0:T(8,128)(2,1)S(1)}, bf16[72,1024]{1,0:T(8,128)(2,1)S(1)}, u32[]{:S(2)}, u32[]{:S(2)}) collective-permute-start(bf16[72,1024]{1,0:T(8,128)(2,1)S(1)} %copy-done.67), channel_id=1, source_target_pairs={{0,2},{2,0},{4,6},{6,4},{8,10},{10,8},{12,14},{14,12},{16,18},{18,... | collective-permute-start | bytes 442376 | tf_op jit(solution)/shard_map/ppermute | solution.py:313
  204.7 5.4 %collective-permute-start.52 = (bf16[72,1024]{1,0:T(8,128)(2,1)S(1)}, bf16[72,1024]{1,0:T(8,128)(2,1)S(1)}, u32[]{:S(2)}, u32[]{:S(2)}) collective-permute-start(bf16[72,1024]{1,0:T(8,128)(2,1)S(1)} %copy-done.63), channel_id=1, source_target_pairs={{0,4},{2,6},{4,0},{6,2},{8,12},{10,14},{12,8},{14,10},{16,20},{18,... | collective-permute-start | bytes 442376 | tf_op jit(solution)/shard_map/ppermute | solution.py:313
  210.1 6.0 %collective-permute-start.53 = (bf16[72,1024]{1,0:T(8,128)(2,1)S(1)}, bf16[72,1024]{1,0:T(8,128)(2,1)S(1)}, u32[]{:S(2)}, u32[]{:S(2)}) collective-permute-start(bf16[72,1024]{1,0:T(8,128)(2,1)S(1)} %copy-done.61), channel_id=1, source_target_pairs={{0,6},{2,4},{4,2},{6,0},{8,14},{10,12},{12,10},{14,8},{16,22},{18,... | collective-permute-start | bytes 442376 | tf_op jit(solution)/shard_map/ppermute | solution.py:313
  216.1 11.4 %collective-permute-start.28 = (bf16[128,1024]{1,0:T(8,128)(2,1)}, bf16[128,1024]{1,0:T(8,128)(2,1)S(1)}, u32[]{:S(2)}, u32[]{:S(2)}) collective-permute-start(bf16[128,1024]{1,0:T(8,128)(2,1)} %expand_rows.5), channel_id=1, source_target_pairs={{0,24},{2,26},{4,28},{6,30},{8,0},{10,2},{12,4},{14,6},{16,8},{18,... | collective-permute-start | bytes 786440 | tf_op jit(solution)/shard_map/ppermute | solution.py:302
  227.5 10.3 %collective-permute-start.50 = (bf16[128,1024]{1,0:T(8,128)(2,1)}, bf16[128,1024]{1,0:T(8,128)(2,1)S(1)}, u32[]{:S(2)}, u32[]{:S(2)}) collective-permute-start(bf16[128,1024]{1,0:T(8,128)(2,1)} %expand_rows.6), channel_id=1, source_target_pairs={{0,16},{2,18},{4,20},{6,22},{8,24},{10,26},{12,28},{14,30},{16,0},... | collective-permute-start | bytes 786440 | tf_op jit(solution)/shard_map/ppermute | solution.py:302
  237.8 8.7 %collective-permute-start.54 = (bf16[128,1024]{1,0:T(8,128)(2,1)}, bf16[128,1024]{1,0:T(8,128)(2,1)S(1)}, u32[]{:S(2)}, u32[]{:S(2)}) collective-permute-start(bf16[128,1024]{1,0:T(8,128)(2,1)} %expand_rows.7), channel_id=1, source_target_pairs={{0,8},{2,10},{4,12},{6,14},{8,16},{10,18},{12,20},{14,22},{16,24},... | collective-permute-start | bytes 786440 | tf_op jit(solution)/shard_map/ppermute | solution.py:302
  (65 other events, 935.0 us)
